TPU v7x, 256 devices: a whole 4x4x8 slice. The times are simulated.
256 devices in a mesh: seq: 64 (over z, y, core), head: 4 (over x).
Axes of the slice: x: 4, y: 4, z: 8, core: 2. Of those that a mesh axis runs over, the one named last changes fastest.
Arguments:
- q_res: bfloat16 [49152, 4096], P('seq', 'head'), may hold values from -6 to 6
- k_res: bfloat16 [49152, 4096], P('seq', 'head'), may hold values from -0.5 to 0.5
- v_res: bfloat16 [49152, 4096], P('seq', 'head'), may hold values from -6 to 6
- q_new: bfloat16 [16384, 4096], P('seq', 'head'), may hold values from -6 to 6
- k_new: bfloat16 [16384, 4096], P('seq', 'head'), may hold values from -0.5 to 0.5
- v_new: bfloat16 [16384, 4096], P('seq', 'head'), may hold values from -6 to 6
- admit_dest: int32 [2048], P('seq'), may hold values from 0 to 63, as said below
- admit_slot: int32 [2048], P('seq'), may hold values from 0 to 31, as said below
- boundaries: int32 [32], replicated, may hold values from 1 to 65535, as said below
- rate: float32 [32], P('head'), may hold values from 0 to 1, as said below
Outputs:
- attended: bfloat16 [65536, 4096], P('seq', 'head')
Inputs may be any that keep to these rules, and one draw needn't show every extreme that they name: `admit_dest`: each shard is named by exactly 32 blocks; the blocks of one shard's new rows name at most 1 times one shard, and exactly 1 times every shard they name. `admit_slot`: every pair of shard and slot is named by exactly one block. `boundaries`: distinct and increasing. `rate`: Positive.
All inputs are finite; a program needn't handle non-finite values.
Results may differ from a plain program's by a relative error of at most 0.0035.
Values may be sent and summed in bfloat16 or wider, within the bound.
A program may use at most 128 MiB of HBM per device.

v0:
```python
import jax
import jax.numpy as jnp
from jax import lax
from jax.sharding import PartitionSpec as P


def prefix(part, axis, combine, identity):
    place = lax.axis_index(axis)
    gathered = jax.tree.map(lambda a: lax.all_gather(a, axis), part)
    state = jax.tree.map(lambda a, e: jnp.zeros_like(a) + jnp.asarray(e, a.dtype), part, identity)

    def one(step, state):
        return combine(
            state, jax.tree.map(lambda a: lax.dynamic_index_in_dim(a, step, 0, False), gathered)
        )

    return lax.fori_loop(0, place, one, state)


def block_pass(carry_state, block, rate):
    q_blk, k_blk, v_blk, r_blk = block
    length = q_blk.shape[0]
    count = jnp.cumsum(r_blk)
    spots = jnp.arange(length).astype(jnp.float32)
    gap = spots[:, None] - spots[None, :]
    linked = (gap >= 0.0) & (count[:, None] == count[None, :])
    decay_mat = jnp.exp(-rate[:, None, None] * jnp.maximum(gap, 0.0)[None, :, :])
    scores = jnp.einsum("ihd,jhd->hij", q_blk, k_blk, preferred_element_type=jnp.float32)
    weights = jnp.where(linked[None, :, :], scores * decay_mat, 0.0).astype(jnp.bfloat16)
    local = jnp.einsum("hij,jhd->ihd", weights, v_blk, preferred_element_type=jnp.float32)
    alive = (count == 0).astype(jnp.float32)
    into = jnp.exp(-rate[None, :] * (spots[:, None] + 1.0)) * alive[:, None]
    carried = jnp.einsum(
        "ihd,hde->ihe",
        q_blk.astype(jnp.float32) * into[:, :, None],
        carry_state,
        precision=lax.Precision.HIGHEST,
    )
    keep = (
        jnp.exp(-rate[None, :] * (length - 1.0 - spots)[:, None])
        * (count == count[-1]).astype(jnp.float32)[:, None]
    )
    fresh = jnp.einsum(
        "jhd,jhe->hde",
        k_blk.astype(jnp.float32) * keep[:, :, None],
        v_blk.astype(jnp.float32),
        precision=lax.Precision.HIGHEST,
    )
    whole = jnp.exp(-rate * length) * alive[-1]
    return (whole[:, None, None] * carry_state + fresh, local + carried)


def attend(q_all, k_all, v_all, reset, rate, start_state, block):
    total, heads, width = q_all.shape
    blocks = total // block
    pieces = (
        q_all.reshape(blocks, block, heads, width),
        k_all.reshape(blocks, block, heads, width),
        v_all.reshape(blocks, block, heads, width),
        reset.reshape(blocks, block),
    )
    end_state, outputs = lax.scan(
        lambda carry, piece: block_pass(carry, piece, rate), start_state, pieces
    )
    return (end_state, outputs.reshape(total, heads, width))


def normalize(output):
    scale = 1.0 / jnp.sqrt(jnp.mean(output * output, axis=-1, keepdims=True) + 1e-06)
    return output * scale


def chain_join(earlier, later):
    return (earlier[0] * later[0], later[0][:, None, None] * earlier[1] + later[1])


def prefix_state(shard_decay, end_state):
    identity = (jnp.ones_like(shard_decay), jnp.zeros_like(end_state))
    joined = prefix((shard_decay, end_state), "seq", chain_join, identity)
    return joined[1]


def body(q_res, k_res, v_res, q_new, k_new, v_new, admit_dest, admit_slot, boundaries, rate):
    shards = lax.axis_size("seq")
    blocks_in = admit_dest.shape[0]
    most = max(1, blocks_in // shards)
    columns = q_res.shape[1]
    unit = q_new.shape[0] // blocks_in
    order = jnp.arange(blocks_in)
    same_dest = admit_dest[:, None] == admit_dest[None, :]
    ahead = order[None, :] < order[:, None]
    rank = jnp.sum((same_dest & ahead).astype(jnp.int32), axis=1)
    target = admit_dest * most + rank
    places = jnp.arange(shards * most)
    match = places[:, None] == target[None, :]
    filled = jnp.any(match, axis=1)
    source = jnp.sum(jnp.where(match, order[None, :], 0), axis=1)
    stacked = jnp.stack([q_new, k_new, v_new]).reshape(3, blocks_in, unit, columns)
    payload = jnp.take(stacked, source, axis=1)
    payload = jnp.where(filled[None, :, None, None], payload, jnp.zeros_like(payload))
    payload = payload.reshape(3, shards, most, unit, columns)
    labels = jnp.where(filled, jnp.take(admit_slot, source) + 1, 0)
    labels = labels.astype(jnp.float32).astype(jnp.bfloat16).reshape(1, shards, most)
    arrived, arrived_labels = (
        lax.all_to_all(payload, "seq", split_axis=1, concat_axis=1, tiled=True),
        lax.all_to_all(labels, "seq", split_axis=1, concat_axis=1, tiled=True),
    )
    slot_of = arrived_labels.reshape(shards * most).astype(jnp.int32) - 1
    pick = jnp.sum(jnp.where(order[:, None] == slot_of[None, :], places[None, :], 0), axis=1)
    admitted = jnp.take(arrived.reshape(3, shards * most, unit, columns), pick, axis=1)
    admitted = admitted.reshape(3, blocks_in * unit, columns)
    heads_here = rate.shape[0]
    width = columns // heads_here
    q_all = jnp.concatenate([q_res, admitted[0]], axis=0)
    k_all = jnp.concatenate([k_res, admitted[1]], axis=0)
    v_all = jnp.concatenate([v_res, admitted[2]], axis=0)
    length = q_all.shape[0]
    q_all = q_all.reshape(length, heads_here, width)
    k_all = k_all.reshape(length, heads_here, width)
    v_all = v_all.reshape(length, heads_here, width)
    where_at = lax.axis_index("seq") * length + jnp.arange(length)
    reset = jnp.any(where_at[:, None] == boundaries[None, :], axis=1).astype(jnp.int32)
    count = jnp.cumsum(reset)
    alive = (count == 0).astype(jnp.float32)
    shard_decay = jnp.exp(-rate * length) * alive[-1]
    spots = jnp.arange(length).astype(jnp.float32)
    block = min(512, length)
    start_state = jnp.zeros((heads_here, width, width), jnp.float32)
    end_state, output = attend(q_all, k_all, v_all, reset, rate, start_state, block)
    incoming = prefix_state(shard_decay, end_state)
    into = jnp.exp(-rate[None, :] * (spots[:, None] + 1.0)) * alive[:, None]
    output = output + jnp.einsum(
        "thd,hde->the",
        q_all.astype(jnp.float32) * into[:, :, None],
        incoming,
        precision=lax.Precision.HIGHEST,
    )
    return normalize(output).reshape(length, columns).astype(jnp.bfloat16)


def solution(mesh):
    in_specs = (
        P("seq", "head"),
        P("seq", "head"),
        P("seq", "head"),
        P("seq", "head"),
        P("seq", "head"),
        P("seq", "head"),
        P("seq"),
        P("seq"),
        P(),
        P("head"),
    )
    out_specs = P("seq", "head")
    return jax.shard_map(body, mesh=mesh, in_specs=in_specs, out_specs=out_specs, check_vma=False)
```

profile of v0, /device:TPU:249, one launch (start us, length us, event | category | flops | bytes accessed | tf_op | source)
XLA Modules:
  0.0 478.2 jit_solution(13515419134812911169)
XLA Ops:
  9.8 9.3 %all-to-all-start = ((bf16[1,64,1]{2,0,1:T(2,128)(2,1)}), bf16[1,64,1]{2,0,1:T(2,128)(2,1)S(1)}, u32[]{:S(2)}, u32[]{:S(2)}) async-start(bf16[1,64,1]{2,0,1:T(2,128)(2,1)} %copy.81), calls=%async_computation | async-start | bytes 65536 | tf_op jit(solution)/shard_map/all_to_all | solution.py:106
  19.2 1.5 pad_maximum_fusion
  20.7 2.4 gather_fusion.1
  23.1 4.0 fusion.33
  27.1 10.4 %all-to-all-start.1 = ((bf16[3,64,1,8,1024]{4,3,0,2,1:T(8,128)(2,1)}), bf16[3,64,1,8,1024]{4,3,0,2,1:T(8,128)(2,1)S(1)}, u32[]{:S(2)}, u32[]{:S(2)}) async-start(bf16[3,64,1,8,1024]{4,3,0,2,1:T(8,128)(2,1)} %fusion.33), calls=%async_computation.1 | async-start | bytes 6291456 | tf_op jit(solution)/shard_map/all_to_all | solution.py:105
  40.9 1.2 add_reduce_fusion
  42.3 64.8 %all-to-all-done.1 = bf16[3,64,1,8,1024]{4,3,0,2,1:T(8,128)(2,1)S(1)} async-done(((bf16[3,64,1,8,1024]{4,3,0,2,1:T(8,128)(2,1)}), bf16[3,64,1,8,1024]{4,3,0,2,1:T(8,128)(2,1)S(1)}, u32[]{:S(2)}, u32[]{:S(2)}) %all-to-all-start.1) | async-done | bytes 3145760 | tf_op jit(solution)/shard_map/all_to_all | solution.py:105
  107.1 2.1 copy.124
  109.1 2.5 gather_fusion.2
  115.6 1.9 copy.104
  117.7 2.0 copy.105
  119.7 122.7 %while.29 = (s32[]{:T(128)}, f32[8,128,128]{2,1,0:T(8,128)}, f32[2,512,8,128]{1,0,3,2:T(2,128)}, f32[8,1,1]{0,2,1:T(1,128)S(1)}, s32[2,512]{1,0:T(2,128)S(1)}, /...) while((s32[]{:T(128)}, f32[8,128,128]{2,1,0:T(8,128)}, ...), condition=%wide.region_8.9_spmd.clone, body=%wide.region_5.8_spmd.clone.sunk | while | flops 2697547776 | bytes 52533776 | solution.py:62
  121.9 2.7 constant_dynamic-slice_fusion.9
  126.8 5.0 %fusion.64 = f32[8,128,512]{2,1,0:T(8,128)S(1)} fusion(f32[512,512]{1,0:T(8,128)} %subtract_maximum_fusion.2, f32[8]{0:T(128)S(1)} %bitcast.171, pred[512,512]{1,0:T(8,128)(4,1)S(1)} %fusion.63, bf16[1,512,8,128]{3,2,1,0:T(8,128)(2,1)} %constant_dynamic-slice_fusion.8, bf16[1,512,8,128]{3,2,1,0:T(8,128)(2,1)} %get-tuple-element.410, ...), kind=kOutput, calls=%fused_computation.6.clone.1 | convolution fusion | flops 1082130432 | bytes 6553632 | tf_op jit(solution)/shard_map/while/body/eval_jaxpr/hij,jhd->ihd/dot_general | solution.py:30
  131.8 2.9 fusion.65
  134.6 2.2 copy.138
  136.8 37.9 %dynamic_update_slice.9 = f32[2,512,8,128]{1,0,3,2:T(2,128)} dynamic-update-slice(f32[2,512,8,128]{1,0,3,2:T(2,128)} %get-tuple-element.426, f32[1,512,8,128]{1,0,3,2:T(1,128)S(1)} %copy.138, s32[]{:T(128)} %get-tuple-element.424, s32[]{:T(128)} %constant.123.clone.1..sunk.1, s32[]{:T(128)} %constant.123.clone.1..sunk.1, s32[]{:T(128)} %constant.123.clone.1..sunk.1) | dynamic-update-slice | bytes 4194308 | tf_op jit(solution)/shard_map/while/body/jit(dynamic_update_index_in_dim)/dynamic_update_slice | solution.py:62
  176.0 4.5 fusion.62
  182.7 2.7 constant_dynamic-slice_fusion.9
  187.6 5.0 %fusion.64 = f32[8,128,512]{2,1,0:T(8,128)S(1)} fusion(f32[512,512]{1,0:T(8,128)} %subtract_maximum_fusion.2, f32[8]{0:T(128)S(1)} %bitcast.171, pred[512,512]{1,0:T(8,128)(4,1)S(1)} %fusion.63, bf16[1,512,8,128]{3,2,1,0:T(8,128)(2,1)} %constant_dynamic-slice_fusion.8, bf16[1,512,8,128]{3,2,1,0:T(8,128)(2,1)} %get-tuple-element.410, ...), kind=kOutput, calls=%fused_computation.6.clone.1 | convolution fusion | flops 1082130432 | bytes 6553632 | tf_op jit(solution)/shard_map/while/body/eval_jaxpr/hij,jhd->ihd/dot_general | solution.py:30
  192.6 3.8 fusion.65
  196.4 2.2 copy.138
  198.6 37.9 %dynamic_update_slice.9 = f32[2,512,8,128]{1,0,3,2:T(2,128)} dynamic-update-slice(f32[2,512,8,128]{1,0,3,2:T(2,128)} %get-tuple-element.426, f32[1,512,8,128]{1,0,3,2:T(1,128)S(1)} %copy.138, s32[]{:T(128)} %get-tuple-element.424, s32[]{:T(128)} %constant.123.clone.1..sunk.1, s32[]{:T(128)} %constant.123.clone.1..sunk.1, s32[]{:T(128)} %constant.123.clone.1..sunk.1) | dynamic-update-slice | bytes 4194308 | tf_op jit(solution)/shard_map/while/body/jit(dynamic_update_index_in_dim)/dynamic_update_slice | solution.py:62
  237.7 4.7 fusion.62
  242.4 125.7 %all-reduce = f32[512]{0:T(512)S(1)} all-reduce(f32[512]{0:T(512)S(1)} %get-tuple-element.305), channel_id=2, replica_groups=mesh['seq'=64,'head'=4] {'seq'}, use_global_device_ids=true, to_apply=%add | all-reduce | flops 512 | bytes 4096
  368.3 1.8 copy_bitcast_fusion.12
  370.1 6.7 %reshape.537 = f32[1024,8,128]{0,2,1:T(8,128)} reshape(f32[2,512,8,128]{1,0,3,2:T(2,128)} %get-tuple-element.173) | data formatting | bytes 8388608 | tf_op jit(solution)/shard_map/reshape | solution.py:65
  377.0 5.9 %all-gather.4.cloned.1.call-done = f32[512,128,128]{2,1,0:T(8,128)} async-done(((f32[8,128,128]{2,1,0:T(8,128)}), f32[512,128,128]{2,1,0:T(8,128)}) %all-gather.4.cloned.1.call-update) | async-done | bytes 33554448 | tf_op jit(solution)/shard_map/all_gather | solution.py:9
  382.9 78.0 %while.28 = (s32[]{:T(128)}, f32[8,128,128]{2,1,0:T(8,128)S(1)}, s32[]{:T(128)}, f32[64,8]{1,0:T(8,128)S(1)}, f32[64,8,128,128]{3,2,1,0:T(8,128)}, /*index=5*/s32[]{:T(128)}, s32[]{:T(128)}, s32[]{:T(128)}) while((s32[]{:T(128)}, f32[8,128,128]{2,1,0:T(8,128)S(1)}, s32[]{:T(128)}, f32[64,8]{1,0:T(8,128)S(1)}, ...), condition=%wide.region_12.13_spmd, body=%wide.region_11.12_spmd.sunk | while | flops 262149 | bytes 1573087 | solution.py:17
  383.0 1.2 bitcast_add_fusion.4
  384.2 1.2 bitcast_add_fusion.4
  385.4 1.2 bitcast_add_fusion.4
  386.7 1.2 bitcast_add_fusion.4
  387.9 1.2 bitcast_add_fusion.4
  389.2 1.2 bitcast_add_fusion.4
  391.6 1.2 bitcast_add_fusion.4
  392.9 1.2 bitcast_add_fusion.4
  394.1 1.2 bitcast_add_fusion.4
  395.4 1.2 bitcast_add_fusion.4
  396.6 1.2 bitcast_add_fusion.4
  397.8 1.2 bitcast_add_fusion.4
  399.1 1.2 bitcast_add_fusion.4
  400.3 1.2 bitcast_add_fusion.4
  401.5 1.2 bitcast_add_fusion.4
  402.8 1.2 bitcast_add_fusion.4
  404.0 1.2 bitcast_add_fusion.4
  405.3 1.2 bitcast_add_fusion.4
  406.5 1.2 bitcast_add_fusion.4
  407.7 1.2 bitcast_add_fusion.4
  409.0 1.2 bitcast_add_fusion.4
  410.2 1.2 bitcast_add_fusion.4
  411.4 1.2 bitcast_add_fusion.4
  412.7 1.2 bitcast_add_fusion.4
  415.2 1.2 bitcast_add_fusion.4
  416.4 1.2 bitcast_add_fusion.4
  417.6 1.2 bitcast_add_fusion.4
  418.9 1.2 bitcast_add_fusion.4
  420.1 1.2 bitcast_add_fusion.4
  421.3 1.2 bitcast_add_fusion.4
  422.6 1.2 bitcast_add_fusion.4
  423.8 1.2 bitcast_add_fusion.4
  425.1 1.2 bitcast_add_fusion.4
  460.9 7.2 %multiply_reduce_fusion = (f32[1024,8]{0,1:T(8,128)S(1)}, f32[1024,8,128]{0,2,1:T(8,128)S(1)}) fusion(f32[1024,8,128]{0,2,1:T(8,128)} %reshape.537, f32[8,128,128]{2,1,0:T(8,128)S(1)} %get-tuple-element.175, bf16[256,8,128]{2,0,1:T(8,128)(2,1)S(1)} %copy.89, bf16[768,8,128]{2,0,1:T(8,128)(2,1)S(1)} %copy_bitcast_fusion.12, ...), kind=kOutput, calls=%fused_computation.50 | convolution fusion | flops 1618993152 | bytes 11075584 | tf_op jit(solution)/shard_map/thd,hde->the/dot_general | solution.py:132
  468.8 2.6 copy.91
  (200 shorter events, 58.5 us)
Async XLA Ops:
  6.5 1.8 copy-start
  9.8 17.3 %all-to-all-start = ((bf16[1,64,1]{2,0,1:T(2,128)(2,1)}), bf16[1,64,1]{2,0,1:T(2,128)(2,1)S(1)}, u32[]{:S(2)}, u32[]{:S(2)}) async-start(bf16[1,64,1]{2,0,1:T(2,128)(2,1)} %copy.81), calls=%async_computation | async-start | bytes 65536 | tf_op jit(solution)/shard_map/all_to_all | solution.py:106
  27.1 10.6 %copy-start.10 = (s32[32]{0:T(128)S(1)}, s32[32]{0:T(128)}, u32[]{:S(2)}) copy-start(s32[32]{0:T(128)} %param.22) | copy-start | bytes 388
  27.1 11.8 %copy-start.11 = (u32[256]{0:T(256)S(1)}, u32[256]{0:T(256)}, u32[]{:S(2)}) copy-start(u32[256]{0:T(256)} %constant.146) | copy-start | bytes 3076
  27.1 13.1 %copy-start.9 = (f32[8]{0:T(128)S(1)}, f32[8]{0:T(128)}, u32[]{:S(2)}) copy-start(f32[8]{0:T(128)} %param.23) | copy-start | bytes 100
  27.1 79.9 %all-to-all-start.1 = ((bf16[3,64,1,8,1024]{4,3,0,2,1:T(8,128)(2,1)}), bf16[3,64,1,8,1024]{4,3,0,2,1:T(8,128)(2,1)S(1)}, u32[]{:S(2)}, u32[]{:S(2)}) async-start(bf16[3,64,1,8,1024]{4,3,0,2,1:T(8,128)(2,1)} %fusion.33), calls=%async_computation.1 | async-start | bytes 6291456 | tf_op jit(solution)/shard_map/all_to_all | solution.py:105
  37.6 345.3 %all-gather.4.cloned.1.call-start = ((), (), s32[]{:S(2)}) async-start(), calls=%async_computation.2 | async-start | bytes 34078720 | tf_op jit(solution)/shard_map/all_gather | solution.py:9
  111.9 1.6 copy-start.7
  111.9 2.1 copy-start.8
  115.6 2.0 copy-start.5
  119.7 4.9 %copy-start.3 = (bf16[2,512,8,128]{3,2,1,0:T(8,128)(2,1)}, bf16[2,512,8,128]{3,2,1,0:T(8,128)(2,1)S(1)}, u32[]{:S(2)}) copy-start(bf16[2,512,8,128]{3,2,1,0:T(8,128)(2,1)S(1)} %get-tuple-element.440) | copy-start | bytes 6291460 | tf_op jit(solution)/shard_map/while
  136.8 39.2 %copy-start.2 = (bf16[1,512,8,128]{3,2,1,0:T(8,128)(2,1)S(1)}, bf16[1,512,8,128]{3,2,1,0:T(8,128)(2,1)}, u32[]{:S(2)}) copy-start(bf16[1,512,8,128]{3,2,1,0:T(8,128)(2,1)} %get-tuple-element.410) | copy-start | bytes 3145732 | tf_op jit(solution)/shard_map/while
  174.8 5.8 %copy-start.4 = (bf16[2,512,8,128]{3,2,1,0:T(8,128)(2,1)S(1)}, bf16[2,512,8,128]{3,2,1,0:T(8,128)(2,1)}, u32[]{:S(2)}) copy-start(bf16[2,512,8,128]{3,2,1,0:T(8,128)(2,1)} %copy-done.3) | copy-start | bytes 6291460 | tf_op jit(solution)/shard_map/while
  180.5 4.9 %copy-start.3 = (bf16[2,512,8,128]{3,2,1,0:T(8,128)(2,1)}, bf16[2,512,8,128]{3,2,1,0:T(8,128)(2,1)S(1)}, u32[]{:S(2)}) copy-start(bf16[2,512,8,128]{3,2,1,0:T(8,128)(2,1)S(1)} %get-tuple-element.440) | copy-start | bytes 6291460 | tf_op jit(solution)/shard_map/while
  198.6 39.2 %copy-start.2 = (bf16[1,512,8,128]{3,2,1,0:T(8,128)(2,1)S(1)}, bf16[1,512,8,128]{3,2,1,0:T(8,128)(2,1)}, u32[]{:S(2)}) copy-start(bf16[1,512,8,128]{3,2,1,0:T(8,128)(2,1)} %get-tuple-element.410) | copy-start | bytes 3145732 | tf_op jit(solution)/shard_map/while
  236.5 5.9 %copy-start.4 = (bf16[2,512,8,128]{3,2,1,0:T(8,128)(2,1)S(1)}, bf16[2,512,8,128]{3,2,1,0:T(8,128)(2,1)}, u32[]{:S(2)}) copy-start(bf16[2,512,8,128]{3,2,1,0:T(8,128)(2,1)} %copy-done.3) | copy-start | bytes 6291460 | tf_op jit(solution)/shard_map/while
  370.1 6.7 %copy-start.6 = (bf16[32,8,8,128]{3,1,2,0:T(8,128)(2,1)S(1)}, bf16[32,8,8,128]{3,1,2,0:T(8,128)(2,1)}, u32[]{:S(2)}) copy-start(bf16[32,8,8,128]{3,1,2,0:T(8,128)(2,1)} %get-tuple-element.296) | copy-start | bytes 1572868
  468.8 2.6 copy-start.1
Sparse Core Ops, SparseCore 0:
  242.5 140.2 all-gather.3
where the time goes:
time: 487 us; the launch traced here: 478 us
  blocking collectives  126 us (26%)
  local copies, waits for them, and re-layouts  119 us (24%)
  other arithmetic  93.2 us (19%)
  waiting for transfers between devices  70.7 us (15%)
  matrix products  33.1 us (7%)
  starting transfers between devices  19.8 us (4%)
  between operations  14.3 us (3%)
    unnamed x1, blocking collectives  126 us
    dynamic_update_slice x4, local copies, waits for them, and re-layouts, attend(): lax.scan(lambda carry, piece: block_pass(carry, piece, rate), start_state...  80.2 us
    add x63, other arithmetic, chain_join(): later[0][:, None, None] * earlier[1] + later[1]  75.1 us
    all_to_all x1, waiting for transfers between devices, body(): lax.all_to_all(payload, 'seq', split_axis=1, concat_axis=1, tiled=True)  64.8 us
    all_to_all x1, starting transfers between devices, body(): lax.all_to_all(payload, 'seq', split_axis=1, concat_axis=1, tiled=True)  10.4 us
    dot_general x2, matrix products, block_pass(): jnp.einsum('hij,jhd->ihd', weights, v_blk, preferred_element_type=jnp.flo...  10 us
  transfers between devices with their start and end apart: 3, of which 2 were waited for; matrix products, arithmetic and copies ran while one was open for 4% of the time, Pallas kernels for 0%

commit v1 on v0

v1 whole, which is shorter than its diff:
```python
import functools

import jax
import jax.numpy as jnp
from jax import lax
from jax.experimental import pallas as pl
from jax.experimental.pallas import tpu as pltpu
from jax.sharding import PartitionSpec as P

MESH = pl.DeviceIdType.MESH
UNIT = 8
PAIR = 2 * UNIT
CHUNK = 256
HD = 128
F32 = jnp.float32
BF16 = jnp.bfloat16
UNFILLED = 4096


def dot(a, b):
    return jnp.dot(a, b, preferred_element_type=F32)


def dot_t(a, b):
    return lax.dot_general(a, b, (((1,), (1,)), ((), ())), preferred_element_type=F32)


def t_dot(a, b):
    return lax.dot_general(a, b, (((0,), (0,)), ((), ())), preferred_element_type=F32)


def two_terms(x):
    high = x.astype(BF16)
    low = (x - high.astype(F32)).astype(BF16)
    return jnp.concatenate([high, low], axis=1)


def fold(x):
    return x[:, :HD] + x[:, HD:]


def kernel(
    n, plane, q_res, k_res, v_res, q_new, k_new, v_new, send_row, labels, b_row, b_col, rate_ref, out,
    q_all, k_all, v_all, kv_stack, q_stack, pay_kv, pay_q, got_kv, got_q, got_labels, place,
    mask, alive, keep, o_local, s_local, end, in1, total, in2, out3, in3,
    load_sem, send_sem, recv_sem, send2, recv2,
):
    me = lax.axis_index("seq")
    z, p = me // plane, lax.rem(me, plane)
    depth = n // plane
    resident = q_res.shape[0]
    length = resident + CHUNK
    chunks = length // CHUNK
    last = chunks - 1
    slots = CHUNK
    columns = q_res.shape[1]
    half = columns // 2

    loads = [
        pltpu.make_async_copy(k_new, kv_stack.at[pl.ds(0, slots)], load_sem.at[0]),
        pltpu.make_async_copy(v_new, kv_stack.at[pl.ds(slots, slots)], load_sem.at[1]),
        pltpu.make_async_copy(q_new.at[:, pl.ds(0, half)], q_stack.at[pl.ds(0, slots)], load_sem.at[2]),
        pltpu.make_async_copy(q_new.at[:, pl.ds(half, half)], q_stack.at[pl.ds(slots, slots)], load_sem.at[3]),
        pltpu.make_async_copy(q_res, q_all.at[pl.ds(0, resident)], load_sem.at[4]),
        pltpu.make_async_copy(k_res, k_all.at[pl.ds(0, resident)], load_sem.at[5]),
        pltpu.make_async_copy(v_res, v_all.at[pl.ds(0, resident)], load_sem.at[6]),
    ]
    for load in loads:
        load.start()

    barrier = pltpu.get_barrier_semaphore()

    def greet(step, carry):
        pl.semaphore_signal(
            barrier, inc=1, device_id={"seq": lax.rem(me + step, n)}, device_id_type=MESH
        )
        return carry

    lax.fori_loop(1, n, greet, 0)

    for load in loads[:4]:
        load.wait()

    def pack(step, carry):
        base = pl.multiple_of(step * 256, 256)
        rows = base + lax.broadcasted_iota(jnp.int32, (256, 2 * slots), 0)
        pick = jnp.where(rows == send_row[...], 1.0, 0.0).astype(BF16)
        for c in range(columns // 256):
            pay_kv[pl.ds(base, 256), pl.ds(c * 256, 256)] = dot(
                pick, kv_stack[:, pl.ds(c * 256, 256)]
            ).astype(BF16)
        for c in range(half // 256):
            pay_q[pl.ds(base, 256), pl.ds(c * 256, 256)] = dot(
                pick, q_stack[:, pl.ds(c * 256, 256)]
            ).astype(BF16)
        return carry

    lax.fori_loop(0, n * PAIR // 256, pack, 0)
    got_kv[pl.ds(0, PAIR)] = pay_kv[pl.ds(0, PAIR)]
    got_q[pl.ds(0, PAIR)] = pay_q[pl.ds(0, PAIR)]
    got_labels[0] = labels[0]

    pl.semaphore_wait(barrier, n - 1)

    def label_copy(step):
        off = lax.rem(step * 37, n)
        return pltpu.make_async_remote_copy(
            src_ref=labels.at[off], dst_ref=got_labels.at[off],
            send_sem=send_sem.at[0], recv_sem=recv_sem.at[0],
            device_id={"seq": lax.rem(me + off, n)}, device_id_type=MESH,
        )

    def kv_copy(step):
        off = lax.rem(step * 37, n)
        rows = pl.ds(pl.multiple_of(off * PAIR, PAIR), PAIR)
        return pltpu.make_async_remote_copy(
            src_ref=pay_kv.at[rows], dst_ref=got_kv.at[rows],
            send_sem=send_sem.at[1], recv_sem=recv_sem.at[1],
            device_id={"seq": lax.rem(me + off, n)}, device_id_type=MESH,
        )

    def q_copy(step):
        off = lax.rem(step * 37, n)
        rows = pl.ds(pl.multiple_of(off * PAIR, PAIR), PAIR)
        return pltpu.make_async_remote_copy(
            src_ref=pay_q.at[rows], dst_ref=got_q.at[rows],
            send_sem=send_sem.at[2], recv_sem=recv_sem.at[2],
            device_id={"seq": lax.rem(me + off, n)}, device_id_type=MESH,
        )

    def start_range(copy, low, high):
        def one(step, carry):
            copy(step).start()
            return carry

        lax.fori_loop(low, high, one, 0)

    start_range(label_copy, 1, n)
    start_range(kv_copy, 1, n)

    rest = pl.ds(PAIR, (n - 1) * PAIR)

    def all_labels():
        return pltpu.make_async_remote_copy(
            src_ref=labels.at[pl.ds(1, n - 1)], dst_ref=got_labels.at[pl.ds(1, n - 1)],
            send_sem=send_sem.at[0], recv_sem=recv_sem.at[0],
            device_id={"seq": lax.rem(me + 1, n)}, device_id_type=MESH,
        )

    def all_kv():
        return pltpu.make_async_remote_copy(
            src_ref=pay_kv.at[rest], dst_ref=got_kv.at[rest],
            send_sem=send_sem.at[1], recv_sem=recv_sem.at[1],
            device_id={"seq": lax.rem(me + 1, n)}, device_id_type=MESH,
        )

    def all_q():
        return pltpu.make_async_remote_copy(
            src_ref=pay_q.at[rest], dst_ref=got_q.at[rest],
            send_sem=send_sem.at[2], recv_sem=recv_sem.at[2],
            device_id={"seq": lax.rem(me + 1, n)}, device_id_type=MESH,
        )

    def clear(low, high):
        inside = (b_row[...] >= low) & (b_row[...] < high)
        found = jnp.sum(jnp.where(inside, 1.0, 0.0), axis=1, keepdims=True)
        return jnp.where(found == 0.0, 1.0, 0.0)

    def starts_upto(position):
        return jnp.sum(jnp.where(b_row[...] <= position, 1.0, 0.0), axis=1, keepdims=True)

    for c in range(chunks):
        base = me * length + c * CHUNK
        spot = base + lax.broadcasted_iota(jnp.int32, (CHUNK, HD), 0)
        count_col = jnp.sum(jnp.where(b_row[...] <= spot, 1.0, 0.0), axis=1, keepdims=True)
        spot_row = base + lax.broadcasted_iota(jnp.int32, (b_col.shape[0], CHUNK), 1)
        b_wide = jnp.concatenate([b_col[...]] * (CHUNK // HD), axis=1)
        count_row = jnp.sum(jnp.where(b_wide <= spot_row, 1.0, 0.0), axis=0, keepdims=True)
        gap = lax.broadcasted_iota(jnp.int32, (CHUNK, CHUNK), 0) - lax.broadcasted_iota(
            jnp.int32, (CHUNK, CHUNK), 1
        )
        mask[c] = jnp.where((gap >= 0) & (count_col == count_row), 1.0, 0.0)
        wide = jnp.broadcast_to(count_col, (CHUNK, HD))
        alive[c] = jnp.where(wide == starts_upto(base - 1), 1.0, 0.0)
        keep[c] = jnp.where(wide == starts_upto(base + CHUNK - 1), 1.0, 0.0)

    def decay_of(x):
        return jnp.exp(jnp.full((1, HD), x, F32))

    def decay_matrix(rate):
        gap = lax.broadcasted_iota(jnp.int32, (CHUNK, CHUNK), 0) - lax.broadcasted_iota(
            jnp.int32, (CHUNK, CHUNK), 1
        )
        return jnp.exp(-rate * jnp.maximum(gap, 0).astype(F32))

    def step_state(c, h, rate, state):
        rows = pl.ds(c * CHUNK, CHUNK)
        cols = pl.ds(pl.multiple_of(h * HD, HD), HD)
        spot = lax.broadcasted_iota(jnp.int32, (CHUNK, HD), 0).astype(F32)
        weight = jnp.exp(-rate * (CHUNK - 1.0 - spot)) * keep[c]
        fresh = fold(t_dot(k_all[rows, cols], two_terms(v_all[rows, cols].astype(F32) * weight)))
        whole = decay_of(-rate * CHUNK) * alive[c, CHUNK - 1 : CHUNK, :]
        return whole * state + fresh

    def local_part(c, h, decay):
        rows = pl.ds(c * CHUNK, CHUNK)
        cols = pl.ds(pl.multiple_of(h * HD, HD), HD)
        scores = dot_t(q_all[rows, cols], k_all[rows, cols])
        weights = (scores * (decay * mask[c])).astype(BF16)
        return dot(weights, v_all[rows, cols])

    for load in loads[4:]:
        load.wait()

    def resident_head(h, carry):
        rate = rate_ref[h]
        decay = decay_matrix(rate)
        cols = pl.ds(pl.multiple_of(h * HD, HD), HD)
        state = jnp.zeros((HD, HD), F32)
        for c in range(last):
            s_local[c, h] = state
            o_local[pl.ds(c * CHUNK, CHUNK), cols] = local_part(c, h, decay)
            state = step_state(c, h, rate, state)
        s_local[last, h] = state
        return carry

    lax.fori_loop(0, plane, resident_head, 0)

    all_labels().wait_recv()
    lane = lax.broadcasted_iota(jnp.int32, (1, HD), 1)
    group = lax.shift_right_logical(lane, 4)
    pieces = []
    for c in range(n * PAIR // HD):
        piece = jnp.zeros((1, HD), jnp.int32)
        for o in range(HD // PAIR):
            piece = piece + jnp.where(group == o, got_labels[c * (HD // PAIR) + o], 0)
        inner = (lane & (UNIT - 1)) + lax.shift_right_logical(lane & UNIT, 3) * slots
        pieces.append(piece + inner)
    for c, piece in enumerate(pieces):
        rows = lax.broadcasted_iota(jnp.int32, (2 * slots, HD), 0)
        place[:, pl.ds(c * HD, HD)] = jnp.where(rows == piece, 1.0, 0.0).astype(BF16)

    start_range(q_copy, 1, n // 4)

    all_kv().wait_recv()

    def arrange_kv(step, carry):
        cols = pl.ds(pl.multiple_of(step * 256, 256), 256)
        whole = dot(place[...], got_kv[:, cols]).astype(BF16)
        k_all[pl.ds(resident, slots), cols] = whole[:slots]
        v_all[pl.ds(resident, slots), cols] = whole[slots:]
        return carry

    lax.fori_loop(0, columns // 256, arrange_kv, 0)

    def end_head(h, carry):
        end[h] = step_state(last, h, rate_ref[h], s_local[last, h])
        return carry

    lax.fori_loop(0, plane, end_head, 0)

    def first_copy(step):
        mate = lax.rem(p + step, plane)
        return pltpu.make_async_remote_copy(
            src_ref=end.at[mate], dst_ref=in1.at[step],
            send_sem=send_sem.at[3], recv_sem=recv_sem.at[3],
            device_id={"seq": z * plane + mate}, device_id_type=MESH,
        )

    def third_copy(step):
        mate = lax.rem(p + step, plane)
        return pltpu.make_async_remote_copy(
            src_ref=out3.at[mate], dst_ref=in3.at[step],
            send_sem=send_sem.at[4], recv_sem=recv_sem.at[4],
            device_id={"seq": z * plane + mate}, device_id_type=MESH,
        )

    def second_copy(step):
        return pltpu.make_async_remote_copy(
            src_ref=total, dst_ref=in2.at[step],
            send_sem=send2.at[step], recv_sem=recv2.at[step],
            device_id={"seq": lax.rem(me + step * plane, n)}, device_id_type=MESH,
        )

    def all_first():
        return pltpu.make_async_remote_copy(
            src_ref=end.at[pl.ds(1, plane - 1)], dst_ref=in1.at[pl.ds(1, plane - 1)],
            send_sem=send_sem.at[3], recv_sem=recv_sem.at[3],
            device_id={"seq": z * plane + lax.rem(p + 1, plane)}, device_id_type=MESH,
        )

    def all_third():
        return pltpu.make_async_remote_copy(
            src_ref=out3.at[pl.ds(1, plane - 1)], dst_ref=in3.at[pl.ds(1, plane - 1)],
            send_sem=send_sem.at[4], recv_sem=recv_sem.at[4],
            device_id={"seq": z * plane + lax.rem(p + 1, plane)}, device_id_type=MESH,
        )

    start_range(first_copy, 1, plane)
    start_range(q_copy, n // 4, n // 2)
    in1[0] = end[p]
    rate_p = rate_ref[p]
    all_first().wait_recv()

    state = jnp.zeros((HD, HD), F32)
    for m in range(plane):
        shard = z * plane + m
        out3[m] = state
        pass_on = decay_of(-rate_p * length) * clear(shard * length, (shard + 1) * length)
        state = pass_on * state + in1[lax.rem(p - m + plane, plane)]
    total[...] = state

    for step in range(1, depth):
        @pl.when(z + step < depth)
        def _(step=step):
            second_copy(step).start()

    start_range(q_copy, n // 2, (3 * n) // 4)

    in2[0] = jnp.zeros((HD, HD), F32)
    span = plane * length
    for step in range(1, depth):
        @pl.when(z - step >= 0)
        def _(step=step):
            second_copy(step).wait_recv()
            factor = decay_of(-rate_p * float(span * (step - 1))) * clear(
                (z - step + 1) * span, z * span
            )
            in2[0] = in2[0] + factor * in2[step]

    before = in2[0]
    for m in range(plane):
        factor = decay_of(-rate_p * float(length * m)) * clear(z * span, z * span + m * length)
        out3[m] = out3[m] + factor * before

    start_range(third_copy, 1, plane)
    start_range(q_copy, (3 * n) // 4, n)
    in3[0] = out3[p]
    all_third().wait_recv()

    def finish(c, h, rate, local):
        rows = pl.ds(c * CHUNK, CHUNK)
        cols = pl.ds(pl.multiple_of(h * HD, HD), HD)
        reach = decay_of(-rate * float(c * CHUNK))
        for m in range(c):
            reach = reach * alive[m, CHUNK - 1 : CHUNK, :]
        carry = s_local[c, h] + reach * in3[lax.rem(p - h + plane, plane)]
        spot = lax.broadcasted_iota(jnp.int32, (CHUNK, HD), 0).astype(F32)
        into = jnp.exp(-rate * (spot + 1.0)) * alive[c]
        whole = local + into * fold(dot(q_all[rows, cols], two_terms(carry)))
        mean = jnp.sum(whole * whole, axis=1, keepdims=True) * (1.0 / HD)
        out[rows, cols] = (whole * lax.rsqrt(mean + 1e-06)).astype(BF16)

    def finish_resident(h, carry):
        rate = rate_ref[h]
        cols = pl.ds(pl.multiple_of(h * HD, HD), HD)
        for c in range(last):
            finish(c, h, rate, o_local[pl.ds(c * CHUNK, CHUNK), cols])
        return carry

    lax.fori_loop(0, plane, finish_resident, 0)

    all_q().wait_recv()

    def arrange_q(step, carry):
        cols = pl.ds(pl.multiple_of(step * 256, 256), 256)
        later = pl.ds(pl.multiple_of(half + step * 256, 256), 256)
        whole = dot(place[...], got_q[:, cols]).astype(BF16)
        q_all[pl.ds(resident, slots), cols] = whole[:slots]
        q_all[pl.ds(resident, slots), later] = whole[slots:]
        return carry

    lax.fori_loop(0, half // 256, arrange_q, 0)

    def finish_admitted(h, carry):
        rate = rate_ref[h]
        finish(last, h, rate, local_part(last, h, decay_matrix(rate)))
        return carry

    lax.fori_loop(0, plane, finish_admitted, 0)

    all_labels().wait_send()
    all_kv().wait_send()
    all_q().wait_send()
    all_first().wait_send()
    all_third().wait_send()
    for step in range(1, depth):
        @pl.when(z + step < depth)
        def _(step=step):
            second_copy(step).wait_send()


def body(q_res, k_res, v_res, q_new, k_new, v_new, admit_dest, admit_slot, boundaries, rate):
    n = lax.axis_size("seq")
    me = lax.axis_index("seq")
    heads = rate.shape[0]
    columns = q_res.shape[1]
    resident, fresh = q_res.shape[0], q_new.shape[0]
    length = resident + fresh
    away = jnp.remainder(admit_dest - me, n)
    inner = jnp.arange(UNIT, dtype=jnp.int32)
    row = (away[:, None] * PAIR + inner[None, :]).reshape(1, fresh)
    send_row = jnp.concatenate([row, row + UNIT], axis=1)
    match = jnp.arange(n, dtype=jnp.int32)[:, None] == away[None, :]
    label = jnp.sum(jnp.where(match, admit_slot[None, :] * UNIT + UNFILLED, 0), axis=1) - UNFILLED
    labels = jnp.broadcast_to(label[:, None, None], (n, 1, HD)).astype(jnp.int32)
    count = boundaries.shape[0]
    b_row = jnp.concatenate([boundaries, jnp.full((HD - count,), 2**30, jnp.int32)]).reshape(1, HD)
    b_col = jnp.broadcast_to(boundaries[:, None], (count, HD))

    any_spec = pl.BlockSpec(memory_space=pl.ANY)
    vmem = pl.BlockSpec(memory_space=pltpu.VMEM)
    smem = pl.BlockSpec(memory_space=pltpu.SMEM)
    chunks = length // CHUNK
    return pl.pallas_call(
        functools.partial(kernel, n, heads),
        out_shape=jax.ShapeDtypeStruct((length, columns), BF16),
        in_specs=[any_spec] * 6 + [vmem] * 4 + [smem],
        out_specs=vmem,
        scratch_shapes=[
            pltpu.VMEM((length, columns), BF16),
            pltpu.VMEM((length, columns), BF16),
            pltpu.VMEM((length, columns), BF16),
            pltpu.VMEM((2 * fresh, columns), BF16),
            pltpu.VMEM((2 * fresh, columns // 2), BF16),
            pltpu.VMEM((n * PAIR, columns), BF16),
            pltpu.VMEM((n * PAIR, columns // 2), BF16),
            pltpu.VMEM((n * PAIR, columns), BF16),
            pltpu.VMEM((n * PAIR, columns // 2), BF16),
            pltpu.VMEM((n, 1, HD), jnp.int32),
            pltpu.VMEM((2 * fresh, n * PAIR), BF16),
            pltpu.VMEM((chunks, CHUNK, CHUNK), F32),
            pltpu.VMEM((chunks, CHUNK, HD), F32),
            pltpu.VMEM((chunks, CHUNK, HD), F32),
            pltpu.VMEM((resident, columns), F32),
            pltpu.VMEM((chunks, heads, HD, HD), F32),
            pltpu.VMEM((heads, HD, HD), F32),
            pltpu.VMEM((heads, HD, HD), F32),
            pltpu.VMEM((HD, HD), F32),
            pltpu.VMEM((n // heads, HD, HD), F32),
            pltpu.VMEM((heads, HD, HD), F32),
            pltpu.VMEM((heads, HD, HD), F32),
            pltpu.SemaphoreType.DMA((7,)),
            pltpu.SemaphoreType.DMA((5,)),
            pltpu.SemaphoreType.DMA((5,)),
            pltpu.SemaphoreType.DMA((n // heads,)),
            pltpu.SemaphoreType.DMA((n // heads,)),
        ],
        compiler_params=pltpu.CompilerParams(
            collective_id=0, has_side_effects=True, vmem_limit_bytes=48 * 1024 * 1024
        ),
    )(q_res, k_res, v_res, q_new, k_new, v_new, send_row, labels, b_row, b_col, rate)


def solution(mesh):
    in_specs = (
        P("seq", "head"),
        P("seq", "head"),
        P("seq", "head"),
        P("seq", "head"),
        P("seq", "head"),
        P("seq", "head"),
        P("seq"),
        P("seq"),
        P(),
        P("head"),
    )
    out_specs = P("seq", "head")
    return jax.shard_map(body, mesh=mesh, in_specs=in_specs, out_specs=out_specs, check_vma=False)
```

time: 487 us -> 123 us (0.25)
  the two profiles are of different devices: /device:TPU:249 before, /device:TPU:2 now
where the time goes in v1:
time: 123 us
  Pallas kernels  111 us (90%)
  local copies, waits for them, and re-layouts  11.3 us (9%)
    pallas_call x1, Pallas kernels, body(): pl.pallas_call(functools.partial(kernel, n, heads), out_shape=jax.ShapeDt...  111 us
    unnamed x13, local copies, waits for them, and re-layouts  9.67 us

profile of v1, /device:TPU:2, one launch (start us, length us, event | category | flops | bytes accessed | tf_op | source)
XLA Modules:
  0.0 122.8 jit_solution(11213259204707755452)
XLA Ops:
  0.0 0.7 pad_bitcast_fusion.b_row
  0.7 0.7 broadcast_multiply_fusion
  1.3 0.1 select_reduce_fusion
  1.4 0.1 iota_add_fusion
  1.5 0.1 add.66
  1.6 0.7 broadcast_in_dim.19.b_col
  2.4 0.1 broadcast_in_dim.18.labels
  2.5 0.0 copy-start
  2.5 1.4 %copy-done = bf16[768,1024]{1,0:T(8,128)(2,1)S(1)} copy-done((bf16[768,1024]{1,0:T(8,128)(2,1)S(1)}, bf16[768,1024]{1,0:T(8,128)(2,1)}, u32[]{:S(2)}) %copy-start) | copy-done | bytes 1572888
  3.9 0.0 copy-start.1
  3.9 1.4 %copy-done.1 = bf16[768,1024]{1,0:T(8,128)(2,1)S(1)} copy-done((bf16[768,1024]{1,0:T(8,128)(2,1)S(1)}, bf16[768,1024]{1,0:T(8,128)(2,1)}, u32[]{:S(2)}) %copy-start.1) | copy-done | bytes 1572888
  5.3 0.0 copy-start.2
  5.3 1.0 copy-done.2
  6.3 0.0 copy-start.3
  6.4 1.0 copy-done.3
  7.4 0.0 copy-start.4
  7.4 1.0 copy-done.4
  8.4 0.0 copy-start.5
  8.4 0.7 copy-done.5
  9.1 110.7 %shard_map.100 = bf16[1024,1024]{1,0:T(8,128)(2,1)} custom-call(bf16[768,1024]{1,0:T(8,128)(2,1)S(1)} %copy-done, bf16[768,1024]{1,0:T(8,128)(2,1)S(1)} %copy-done.1, bf16[768,1024]{1,0:T(8,128)(2,1)} %v_res.1, bf16[256,1024]{1,0:T(8,128)(2,1)S(1)} %copy-done.2, bf16[256,1024]{1,0:T(8,128)(2,1)S(1)} %copy-done.3, bf16[256,1024]{1,0:T(8,128)(2,1)S(1)} %copy-done.4, ...), custom_call_target="tpu_custom_call" | custom-call | tf_op jit(solution)/shard_map/pallas_call | solution.py:415
  119.7 3.1 %copy.12 = bf16[1024,1024]{1,0:T(8,128)(2,1)} copy(bf16[1024,1024]{1,0:T(8,128)(2,1)} %shard_map.100) | data formatting | bytes 4194304
  (3 shorter events, 0.0 us)
Async XLA Ops:
  2.5 1.4 %copy-start = (bf16[768,1024]{1,0:T(8,128)(2,1)S(1)}, bf16[768,1024]{1,0:T(8,128)(2,1)}, u32[]{:S(2)}) copy-start(bf16[768,1024]{1,0:T(8,128)(2,1)} %q_res.1) | copy-start | bytes 4718596
  3.9 1.4 %copy-start.1 = (bf16[768,1024]{1,0:T(8,128)(2,1)S(1)}, bf16[768,1024]{1,0:T(8,128)(2,1)}, u32[]{:S(2)}) copy-start(bf16[768,1024]{1,0:T(8,128)(2,1)} %k_res.1) | copy-start | bytes 4718596
  5.3 1.0 copy-start.2
  6.3 1.0 copy-start.3
  7.4 1.0 copy-start.4
  8.4 0.7 copy-start.5

commit v2 on v1

--- a/solution.py
+++ b/solution.py
@@ -15,6 +15,7 @@
 F32 = jnp.float32
 BF16 = jnp.bfloat16
 UNFILLED = 4096
+STRIDE = 37
 
 
 def dot(a, b):
@@ -42,8 +43,8 @@
 def kernel(
     n, plane, q_res, k_res, v_res, q_new, k_new, v_new, send_row, labels, b_row, b_col, rate_ref, out,
     q_all, k_all, v_all, kv_stack, q_stack, pay_kv, pay_q, got_kv, got_q, got_labels, place,
-    mask, alive, keep, o_local, s_local, end, in1, total, in2, out3, in3,
-    load_sem, send_sem, recv_sem, send2, recv2,
+    mask, alive, keep, o_local, s_local, end, in1, total, in2, before, out3, in3, done,
+    load_sem, send_sem, recv_sem, send2, recv2, out_sem,
 ):
     me = lax.axis_index("seq")
     z, p = me // plane, lax.rem(me, plane)
@@ -78,54 +79,30 @@
 
     lax.fori_loop(1, n, greet, 0)
 
-    for load in loads[:4]:
-        load.wait()
-
-    def pack(step, carry):
-        base = pl.multiple_of(step * 256, 256)
-        rows = base + lax.broadcasted_iota(jnp.int32, (256, 2 * slots), 0)
-        pick = jnp.where(rows == send_row[...], 1.0, 0.0).astype(BF16)
-        for c in range(columns // 256):
-            pay_kv[pl.ds(base, 256), pl.ds(c * 256, 256)] = dot(
-                pick, kv_stack[:, pl.ds(c * 256, 256)]
-            ).astype(BF16)
-        for c in range(half // 256):
-            pay_q[pl.ds(base, 256), pl.ds(c * 256, 256)] = dot(
-                pick, q_stack[:, pl.ds(c * 256, 256)]
-            ).astype(BF16)
-        return carry
-
-    lax.fori_loop(0, n * PAIR // 256, pack, 0)
-    got_kv[pl.ds(0, PAIR)] = pay_kv[pl.ds(0, PAIR)]
-    got_q[pl.ds(0, PAIR)] = pay_q[pl.ds(0, PAIR)]
-    got_labels[0] = labels[0]
-
-    pl.semaphore_wait(barrier, n - 1)
+    def ahead(step):
+        return lax.rem(me + step * STRIDE, n)
 
     def label_copy(step):
-        off = lax.rem(step * 37, n)
-        return pltpu.make_async_remote_copy(
-            src_ref=labels.at[off], dst_ref=got_labels.at[off],
+        return pltpu.make_async_remote_copy(
+            src_ref=labels.at[step], dst_ref=got_labels.at[step],
             send_sem=send_sem.at[0], recv_sem=recv_sem.at[0],
-            device_id={"seq": lax.rem(me + off, n)}, device_id_type=MESH,
+            device_id={"seq": ahead(step)}, device_id_type=MESH,
         )
 
     def kv_copy(step):
-        off = lax.rem(step * 37, n)
-        rows = pl.ds(pl.multiple_of(off * PAIR, PAIR), PAIR)
+        rows = pl.ds(pl.multiple_of(step * PAIR, PAIR), PAIR)
         return pltpu.make_async_remote_copy(
             src_ref=pay_kv.at[rows], dst_ref=got_kv.at[rows],
             send_sem=send_sem.at[1], recv_sem=recv_sem.at[1],
-            device_id={"seq": lax.rem(me + off, n)}, device_id_type=MESH,
+            device_id={"seq": ahead(step)}, device_id_type=MESH,
         )
 
     def q_copy(step):
-        off = lax.rem(step * 37, n)
-        rows = pl.ds(pl.multiple_of(off * PAIR, PAIR), PAIR)
+        rows = pl.ds(pl.multiple_of(step * PAIR, PAIR), PAIR)
         return pltpu.make_async_remote_copy(
             src_ref=pay_q.at[rows], dst_ref=got_q.at[rows],
             send_sem=send_sem.at[2], recv_sem=recv_sem.at[2],
-            device_id={"seq": lax.rem(me + off, n)}, device_id_type=MESH,
+            device_id={"seq": ahead(step)}, device_id_type=MESH,
         )
 
     def start_range(copy, low, high):
@@ -135,8 +112,44 @@
 
         lax.fori_loop(low, high, one, 0)
 
+    def pick(base):
+        rows = base + lax.broadcasted_iota(jnp.int32, (256, 2 * slots), 0)
+        return jnp.where(rows == send_row[...], 1.0, 0.0).astype(BF16)
+
+    def pack_kv(base):
+        chosen = pick(base)
+        for c in range(columns // 256):
+            pay_kv[pl.ds(base, 256), pl.ds(c * 256, 256)] = dot(
+                chosen, kv_stack[:, pl.ds(c * 256, 256)]
+            ).astype(BF16)
+
+    for load in loads[:2]:
+        load.wait()
+    pack_kv(0)
+    pl.semaphore_wait(barrier, n - 1)
+    group = 256 // PAIR
+    start_range(kv_copy, 1, group)
     start_range(label_copy, 1, n)
-    start_range(kv_copy, 1, n)
+    for part in range(1, n // group):
+        pack_kv(part * 256)
+        start_range(kv_copy, part * group, (part + 1) * group)
+
+    for load in loads[2:4]:
+        load.wait()
+
+    def pack_q(step, carry):
+        base = pl.multiple_of(step * 256, 256)
+        chosen = pick(base)
+        for c in range(half // 256):
+            pay_q[pl.ds(base, 256), pl.ds(c * 256, 256)] = dot(
+                chosen, q_stack[:, pl.ds(c * 256, 256)]
+            ).astype(BF16)
+        return carry
+
+    lax.fori_loop(0, n // group, pack_q, 0)
+    got_kv[pl.ds(0, PAIR)] = pay_kv[pl.ds(0, PAIR)]
+    got_q[pl.ds(0, PAIR)] = pay_q[pl.ds(0, PAIR)]
+    got_labels[0] = labels[0]
 
     rest = pl.ds(PAIR, (n - 1) * PAIR)
 
@@ -228,12 +241,12 @@
 
     all_labels().wait_recv()
     lane = lax.broadcasted_iota(jnp.int32, (1, HD), 1)
-    group = lax.shift_right_logical(lane, 4)
+    owner = lax.shift_right_logical(lane, 4)
     pieces = []
     for c in range(n * PAIR // HD):
         piece = jnp.zeros((1, HD), jnp.int32)
         for o in range(HD // PAIR):
-            piece = piece + jnp.where(group == o, got_labels[c * (HD // PAIR) + o], 0)
+            piece = piece + jnp.where(owner == o, got_labels[c * (HD // PAIR) + o], 0)
         inner = (lane & (UNIT - 1)) + lax.shift_right_logical(lane & UNIT, 3) * slots
         pieces.append(piece + inner)
     for c, piece in enumerate(pieces):
@@ -253,12 +266,6 @@
 
     lax.fori_loop(0, columns // 256, arrange_kv, 0)
 
-    def end_head(h, carry):
-        end[h] = step_state(last, h, rate_ref[h], s_local[last, h])
-        return carry
-
-    lax.fori_loop(0, plane, end_head, 0)
-
     def first_copy(step):
         mate = lax.rem(p + step, plane)
         return pltpu.make_async_remote_copy(
@@ -296,8 +303,17 @@
             device_id={"seq": z * plane + lax.rem(p + 1, plane)}, device_id_type=MESH,
         )
 
-    start_range(first_copy, 1, plane)
+    def end_head(h):
+        end[h] = step_state(last, h, rate_ref[h], s_local[last, h])
+
+    def end_mate(step, carry):
+        end_head(lax.rem(p + step, plane))
+        first_copy(step).start()
+        return carry
+
+    lax.fori_loop(1, plane, end_mate, 0)
     start_range(q_copy, n // 4, n // 2)
+    end_head(p)
     in1[0] = end[p]
     rate_p = rate_ref[p]
     all_first().wait_recv()
@@ -308,7 +324,7 @@
         out3[m] = state
         pass_on = decay_of(-rate_p * length) * clear(shard * length, (shard + 1) * length)
         state = pass_on * state + in1[lax.rem(p - m + plane, plane)]
-    total[...] = state
+    total[...] = state.astype(BF16)
 
     for step in range(1, depth):
         @pl.when(z + step < depth)
@@ -317,7 +333,7 @@
 
     start_range(q_copy, n // 2, (3 * n) // 4)
 
-    in2[0] = jnp.zeros((HD, HD), F32)
+    before[...] = jnp.zeros((HD, HD), F32)
     span = plane * length
     for step in range(1, depth):
         @pl.when(z - step >= 0)
@@ -326,12 +342,12 @@
             factor = decay_of(-rate_p * float(span * (step - 1))) * clear(
                 (z - step + 1) * span, z * span
             )
-            in2[0] = in2[0] + factor * in2[step]
-
-    before = in2[0]
+            before[...] = before[...] + factor * in2[step].astype(F32)
+
+    earlier = before[...]
     for m in range(plane):
         factor = decay_of(-rate_p * float(length * m)) * clear(z * span, z * span + m * length)
-        out3[m] = out3[m] + factor * before
+        out3[m] = out3[m] + factor * earlier
 
     start_range(third_copy, 1, plane)
     start_range(q_copy, (3 * n) // 4, n)
@@ -349,7 +365,7 @@
         into = jnp.exp(-rate * (spot + 1.0)) * alive[c]
         whole = local + into * fold(dot(q_all[rows, cols], two_terms(carry)))
         mean = jnp.sum(whole * whole, axis=1, keepdims=True) * (1.0 / HD)
-        out[rows, cols] = (whole * lax.rsqrt(mean + 1e-06)).astype(BF16)
+        done[rows, cols] = (whole * lax.rsqrt(mean + 1e-06)).astype(BF16)
 
     def finish_resident(h, carry):
         rate = rate_ref[h]
@@ -358,7 +374,11 @@
             finish(c, h, rate, o_local[pl.ds(c * CHUNK, CHUNK), cols])
         return carry
 
-    lax.fori_loop(0, plane, finish_resident, 0)
+    lax.fori_loop(0, plane, finish_resident, 0, unroll=2)
+    rows_in = pl.ds(0, resident)
+    rows_new = pl.ds(resident, slots)
+    store = pltpu.make_async_copy(done.at[rows_in], out.at[rows_in], out_sem.at[0])
+    store.start()
 
     all_q().wait_recv()
 
@@ -377,7 +397,9 @@
         finish(last, h, rate, local_part(last, h, decay_matrix(rate)))
         return carry
 
-    lax.fori_loop(0, plane, finish_admitted, 0)
+    lax.fori_loop(0, plane, finish_admitted, 0, unroll=2)
+    store_new = pltpu.make_async_copy(done.at[rows_new], out.at[rows_new], out_sem.at[1])
+    store_new.start()
 
     all_labels().wait_send()
     all_kv().wait_send()
@@ -388,6 +410,20 @@
         @pl.when(z + step < depth)
         def _(step=step):
             second_copy(step).wait_send()
+    store.wait()
+    store_new.wait()
+
+
+def hand_over(parts, src, dst, sem):
+    size = src.shape[0] // parts
+    copies = [
+        pltpu.make_async_copy(src.at[pl.ds(i * size, size)], dst.at[pl.ds(i * size, size)], sem.at[i])
+        for i in range(parts)
+    ]
+    for copy in copies:
+        copy.start()
+    for copy in copies:
+        copy.wait()
 
 
 def body(q_res, k_res, v_res, q_new, k_new, v_new, admit_dest, admit_slot, boundaries, rate):
@@ -399,9 +435,10 @@
     length = resident + fresh
     away = jnp.remainder(admit_dest - me, n)
     inner = jnp.arange(UNIT, dtype=jnp.int32)
-    row = (away[:, None] * PAIR + inner[None, :]).reshape(1, fresh)
+    slot = jnp.remainder(away * pow(STRIDE, -1, n), n)
+    row = (slot[:, None] * PAIR + inner[None, :]).reshape(1, fresh)
     send_row = jnp.concatenate([row, row + UNIT], axis=1)
-    match = jnp.arange(n, dtype=jnp.int32)[:, None] == away[None, :]
+    match = jnp.arange(n, dtype=jnp.int32)[:, None] == slot[None, :]
     label = jnp.sum(jnp.where(match, admit_slot[None, :] * UNIT + UNFILLED, 0), axis=1) - UNFILLED
     labels = jnp.broadcast_to(label[:, None, None], (n, 1, HD)).astype(jnp.int32)
     count = boundaries.shape[0]
@@ -412,11 +449,11 @@
     vmem = pl.BlockSpec(memory_space=pltpu.VMEM)
     smem = pl.BlockSpec(memory_space=pltpu.SMEM)
     chunks = length // CHUNK
-    return pl.pallas_call(
+    result = pl.pallas_call(
         functools.partial(kernel, n, heads),
         out_shape=jax.ShapeDtypeStruct((length, columns), BF16),
         in_specs=[any_spec] * 6 + [vmem] * 4 + [smem],
-        out_specs=vmem,
+        out_specs=any_spec,
         scratch_shapes=[
             pltpu.VMEM((length, columns), BF16),
             pltpu.VMEM((length, columns), BF16),
@@ -436,20 +473,32 @@
             pltpu.VMEM((chunks, heads, HD, HD), F32),
             pltpu.VMEM((heads, HD, HD), F32),
             pltpu.VMEM((heads, HD, HD), F32),
+            pltpu.VMEM((HD, HD), BF16),
+            pltpu.VMEM((n // heads, HD, HD), BF16),
             pltpu.VMEM((HD, HD), F32),
-            pltpu.VMEM((n // heads, HD, HD), F32),
             pltpu.VMEM((heads, HD, HD), F32),
             pltpu.VMEM((heads, HD, HD), F32),
+            pltpu.VMEM((length, columns), BF16),
             pltpu.SemaphoreType.DMA((7,)),
             pltpu.SemaphoreType.DMA((5,)),
             pltpu.SemaphoreType.DMA((5,)),
             pltpu.SemaphoreType.DMA((n // heads,)),
             pltpu.SemaphoreType.DMA((n // heads,)),
+            pltpu.SemaphoreType.DMA((2,)),
         ],
         compiler_params=pltpu.CompilerParams(
-            collective_id=0, has_side_effects=True, vmem_limit_bytes=48 * 1024 * 1024
+            collective_id=0, has_side_effects=True, vmem_limit_bytes=60 * 1024 * 1024
         ),
     )(q_res, k_res, v_res, q_new, k_new, v_new, send_row, labels, b_row, b_col, rate)
+    parts = 4
+    return pl.pallas_call(
+        functools.partial(hand_over, parts),
+        out_shape=jax.ShapeDtypeStruct((length, columns), BF16),
+        in_specs=[any_spec],
+        out_specs=any_spec,
+        scratch_shapes=[pltpu.SemaphoreType.DMA((parts,))],
+        compiler_params=pltpu.CompilerParams(vmem_limit_bytes=60 * 1024 * 1024),
+    )(result)
 
 
 def solution(mesh):

time: 123 us -> 169 us (1.37)
  the two profiles are of different devices: /device:TPU:2 before, /device:TPU:1 now
where the time goes in v2:
time: 169 us; the launch traced here: 167 us
  Pallas kernels  162 us (96%)
  local copies, waits for them, and re-layouts  3.33 us (2%)
    pallas_call x1, Pallas kernels, body(): pl.pallas_call(functools.partial(kernel, n, heads), out_shape=jax.ShapeDt...  97.7 us
    pallas_call x1, Pallas kernels, body(): pl.pallas_call(functools.partial(hand_over, parts), out_shape=jax.ShapeDt...  64.7 us

profile of v2, /device:TPU:1, one launch (start us, length us, event | category | flops | bytes accessed | tf_op | source)
XLA Modules:
  0.0 167.2 jit_solution(13682437888657971026)
XLA Ops:
  0.0 1.2 pad_bitcast_fusion.b_row
  1.2 0.7 broadcast_multiply_fusion
  1.9 0.1 select_reduce_fusion
  2.0 0.1 iota_add_fusion
  2.0 0.1 add.71
  2.1 0.6 pad_add_fusion.send_row
  2.7 1.3 broadcast_in_dim.19.b_col
  4.0 0.7 broadcast_in_dim.18.labels
  4.8 97.7 %shard_map.100.src = bf16[1024,1024]{1,0:T(8,128)(2,1)} custom-call(bf16[768,1024]{1,0:T(8,128)(2,1)} %q_res.1, bf16[768,1024]{1,0:T(8,128)(2,1)} %k_res.1, bf16[768,1024]{1,0:T(8,128)(2,1)} %v_res.1, bf16[256,1024]{1,0:T(8,128)(2,1)} %q_new.1, bf16[256,1024]{1,0:T(8,128)(2,1)} %k_new.1, bf16[256,1024]{1,0:T(8,128)(2,1)} %v_new.1, ...), custom_call_target="tpu_custom_call" | custom-call | tf_op jit(solution)/shard_map/pallas_call | solution.py:452
  102.5 64.7 %shard_map.101 = bf16[1024,1024]{1,0:T(8,128)(2,1)} custom-call(bf16[1024,1024]{1,0:T(8,128)(2,1)} %shard_map.100.src), custom_call_target="tpu_custom_call" | custom-call | tf_op jit(solution)/shard_map/pallas_call | solution.py:494
  (2 shorter events, 0.0 us)

commit v3 on v2

--- a/solution.py
+++ b/solution.py
@@ -41,7 +41,8 @@
 
 
 def kernel(
-    n, plane, q_res, k_res, v_res, q_new, k_new, v_new, send_row, labels, b_row, b_col, rate_ref, out,
+    n, plane, q_res, k_res, v_res, q_new, k_new, v_new, dest_ref, slot_ref, bound_ref, rate_ref, out,
+    send_row, labels, b_row, b_col,
     q_all, k_all, v_all, kv_stack, q_stack, pay_kv, pay_q, got_kv, got_q, got_labels, place,
     mask, alive, keep, o_local, s_local, end, in1, total, in2, before, out3, in3, done,
     load_sem, send_sem, recv_sem, send2, recv2, out_sem,
@@ -79,8 +80,23 @@
 
     lax.fori_loop(1, n, greet, 0)
 
+    side = 1 - 2 * lax.rem(me, 2)
+
     def ahead(step):
-        return lax.rem(me + step * STRIDE, n)
+        return lax.rem(me + n * STRIDE + side * step * STRIDE, n)
+
+    blocks_in = dest_ref.shape[0]
+    back = pow(STRIDE, -1, n)
+    lane = lax.broadcasted_iota(jnp.int32, (1, 2 * slots), 1)
+    unit = lax.rem(lax.shift_right_logical(lane, 3), blocks_in)
+    row = jnp.zeros((1, 2 * slots), jnp.int32)
+    label = jnp.full((n, HD), -UNFILLED, jnp.int32)
+    label_row = lax.broadcasted_iota(jnp.int32, (n, HD), 0)
+    for u in range(blocks_in):
+        slot = lax.rem((dest_ref[u] - me) * side * back + n * n, n)
+        row = jnp.where(unit == u, slot * PAIR, row)
+        label = jnp.where(label_row == slot, slot_ref[u] * UNIT, label)
+    send_row[...] = row + (lane & (UNIT - 1)) + (lane // slots) * UNIT
 
     def label_copy(step):
         return pltpu.make_async_remote_copy(
@@ -129,6 +145,8 @@
     pl.semaphore_wait(barrier, n - 1)
     group = 256 // PAIR
     start_range(kv_copy, 1, group)
+    for step in range(n):
+        labels[step] = label[step : step + 1, :]
     start_range(label_copy, 1, n)
     for part in range(1, n // group):
         pack_kv(part * 256)
@@ -173,6 +191,17 @@
             send_sem=send_sem.at[2], recv_sem=recv_sem.at[2],
             device_id={"seq": lax.rem(me + 1, n)}, device_id_type=MESH,
         )
+
+    count = bound_ref.shape[0]
+    across = lax.broadcasted_iota(jnp.int32, (1, HD), 1)
+    down = lax.broadcasted_iota(jnp.int32, (count, HD), 0)
+    line = jnp.full((1, HD), 2**30, jnp.int32)
+    column = jnp.full((count, HD), 2**30, jnp.int32)
+    for j in range(count):
+        line = jnp.where(across == j, bound_ref[j], line)
+        column = jnp.where(down == j, bound_ref[j], column)
+    b_row[...] = line
+    b_col[...] = column
 
     def clear(low, high):
         inside = (b_row[...] >= low) & (b_row[...] < high)
@@ -414,47 +443,46 @@
     store_new.wait()
 
 
-def hand_over(parts, src, dst, sem):
+def hand_over(parts, src, dst, hold, load_sem, store_sem):
     size = src.shape[0] // parts
-    copies = [
-        pltpu.make_async_copy(src.at[pl.ds(i * size, size)], dst.at[pl.ds(i * size, size)], sem.at[i])
-        for i in range(parts)
+    pieces = [pl.ds(i * size, size) for i in range(parts)]
+    loads = [
+        pltpu.make_async_copy(src.at[rows], hold.at[rows], load_sem.at[i])
+        for i, rows in enumerate(pieces)
     ]
-    for copy in copies:
-        copy.start()
-    for copy in copies:
-        copy.wait()
+    stores = [
+        pltpu.make_async_copy(hold.at[rows], dst.at[rows], store_sem.at[i])
+        for i, rows in enumerate(pieces)
+    ]
+    for load in loads:
+        load.start()
+    for load, store in zip(loads, stores):
+        load.wait()
+        store.start()
+    for store in stores:
+        store.wait()
 
 
 def body(q_res, k_res, v_res, q_new, k_new, v_new, admit_dest, admit_slot, boundaries, rate):
     n = lax.axis_size("seq")
-    me = lax.axis_index("seq")
     heads = rate.shape[0]
     columns = q_res.shape[1]
     resident, fresh = q_res.shape[0], q_new.shape[0]
     length = resident + fresh
-    away = jnp.remainder(admit_dest - me, n)
-    inner = jnp.arange(UNIT, dtype=jnp.int32)
-    slot = jnp.remainder(away * pow(STRIDE, -1, n), n)
-    row = (slot[:, None] * PAIR + inner[None, :]).reshape(1, fresh)
-    send_row = jnp.concatenate([row, row + UNIT], axis=1)
-    match = jnp.arange(n, dtype=jnp.int32)[:, None] == slot[None, :]
-    label = jnp.sum(jnp.where(match, admit_slot[None, :] * UNIT + UNFILLED, 0), axis=1) - UNFILLED
-    labels = jnp.broadcast_to(label[:, None, None], (n, 1, HD)).astype(jnp.int32)
     count = boundaries.shape[0]
-    b_row = jnp.concatenate([boundaries, jnp.full((HD - count,), 2**30, jnp.int32)]).reshape(1, HD)
-    b_col = jnp.broadcast_to(boundaries[:, None], (count, HD))
-
     any_spec = pl.BlockSpec(memory_space=pl.ANY)
-    vmem = pl.BlockSpec(memory_space=pltpu.VMEM)
     smem = pl.BlockSpec(memory_space=pltpu.SMEM)
     chunks = length // CHUNK
     result = pl.pallas_call(
         functools.partial(kernel, n, heads),
         out_shape=jax.ShapeDtypeStruct((length, columns), BF16),
-        in_specs=[any_spec] * 6 + [vmem] * 4 + [smem],
+        in_specs=[any_spec] * 6 + [smem] * 4,
         out_specs=any_spec,
         scratch_shapes=[
+            pltpu.VMEM((1, 2 * fresh), jnp.int32),
+            pltpu.VMEM((n, 1, HD), jnp.int32),
+            pltpu.VMEM((1, HD), jnp.int32),
+            pltpu.VMEM((count, HD), jnp.int32),
             pltpu.VMEM((length, columns), BF16),
             pltpu.VMEM((length, columns), BF16),
             pltpu.VMEM((length, columns), BF16),
@@ -489,14 +517,18 @@
         compiler_params=pltpu.CompilerParams(
             collective_id=0, has_side_effects=True, vmem_limit_bytes=60 * 1024 * 1024
         ),
-    )(q_res, k_res, v_res, q_new, k_new, v_new, send_row, labels, b_row, b_col, rate)
-    parts = 4
+    )(q_res, k_res, v_res, q_new, k_new, v_new, admit_dest, admit_slot, boundaries, rate)
+    parts = 8
     return pl.pallas_call(
         functools.partial(hand_over, parts),
         out_shape=jax.ShapeDtypeStruct((length, columns), BF16),
         in_specs=[any_spec],
         out_specs=any_spec,
-        scratch_shapes=[pltpu.SemaphoreType.DMA((parts,))],
+        scratch_shapes=[
+            pltpu.VMEM((length, columns), BF16),
+            pltpu.SemaphoreType.DMA((parts,)),
+            pltpu.SemaphoreType.DMA((parts,)),
+        ],
         compiler_params=pltpu.CompilerParams(vmem_limit_bytes=60 * 1024 * 1024),
     )(result)
 

time: 169 us -> 100 us (0.59)
  Pallas kernels: 162 us -> 99.6 us
  local copies, waits for them, and re-layouts: 3.33 us -> 0 us
    pallas_call x1, Pallas kernels: 64.7 us -> 2.39 us  [body(): pl.pallas_call(functools.partial(hand_over, parts), out_shape=jax.ShapeDt...]
    broadcast_in_dim x2 -> x0, local copies, waits for them, and re-layouts: 2.07 us -> none  [the longest x1 1.32 us: body(): b_col = jnp.broadcast_to(boundaries[:, None], (count, HD))]
where the time goes in v3:
time: 100 us; the launch traced here: 99.6 us
  Pallas kernels  99.6 us (100%)
    pallas_call x1, Pallas kernels, body(): pl.pallas_call(functools.partial(kernel, n, heads), out_shape=jax.ShapeDt...  97.2 us
    pallas_call x1, Pallas kernels, body(): pl.pallas_call(functools.partial(hand_over, parts), out_shape=jax.ShapeDt...  2.39 us

profile of v3, /device:TPU:1, one launch (start us, length us, event | category | flops | bytes accessed | tf_op | source)
XLA Modules:
  0.0 99.6 jit_solution(5137564780637450060)
XLA Ops:
  0.0 97.2 %shard_map.100.src = bf16[1024,1024]{1,0:T(8,128)(2,1)} custom-call(bf16[768,1024]{1,0:T(8,128)(2,1)} %q_res.1, bf16[768,1024]{1,0:T(8,128)(2,1)} %k_res.1, bf16[768,1024]{1,0:T(8,128)(2,1)} %v_res.1, bf16[256,1024]{1,0:T(8,128)(2,1)} %q_new.1, bf16[256,1024]{1,0:T(8,128)(2,1)} %k_new.1, bf16[256,1024]{1,0:T(8,128)(2,1)} %v_new.1, s32[32]{0:T(128)} %dest_ref.1, ...), custom_call_target="tpu_custom_call" | custom-call | tf_op jit(solution)/shard_map/pallas_call | solution.py:476
  97.2 2.4 %shard_map.101 = bf16[1024,1024]{1,0:T(8,128)(2,1)} custom-call(bf16[1024,1024]{1,0:T(8,128)(2,1)} %shard_map.100.src), custom_call_target="tpu_custom_call" | custom-call | tf_op jit(solution)/shard_map/pallas_call | solution.py:522

commit v4 on v3

--- a/solution.py
+++ b/solution.py
@@ -16,6 +16,7 @@
 BF16 = jnp.bfloat16
 UNFILLED = 4096
 STRIDE = 37
+GROUPS = 2
 
 
 def dot(a, b):
@@ -57,6 +58,9 @@
     slots = CHUNK
     columns = q_res.shape[1]
     half = columns // 2
+    span = columns // GROUPS
+    heads_in = plane // GROUPS
+    piece_rows = HD // GROUPS
 
     loads = [
         pltpu.make_async_copy(k_new, kv_stack.at[pl.ds(0, slots)], load_sem.at[0]),
@@ -105,11 +109,11 @@
             device_id={"seq": ahead(step)}, device_id_type=MESH,
         )
 
-    def kv_copy(step):
+    def kv_copy(g, step):
         rows = pl.ds(pl.multiple_of(step * PAIR, PAIR), PAIR)
         return pltpu.make_async_remote_copy(
-            src_ref=pay_kv.at[rows], dst_ref=got_kv.at[rows],
-            send_sem=send_sem.at[1], recv_sem=recv_sem.at[1],
+            src_ref=pay_kv.at[g, rows], dst_ref=got_kv.at[g, rows],
+            send_sem=send_sem.at[4 + g], recv_sem=recv_sem.at[4 + g],
             device_id={"seq": ahead(step)}, device_id_type=MESH,
         )
 
@@ -117,7 +121,7 @@
         rows = pl.ds(pl.multiple_of(step * PAIR, PAIR), PAIR)
         return pltpu.make_async_remote_copy(
             src_ref=pay_q.at[rows], dst_ref=got_q.at[rows],
-            send_sem=send_sem.at[2], recv_sem=recv_sem.at[2],
+            send_sem=send_sem.at[1], recv_sem=recv_sem.at[1],
             device_id={"seq": ahead(step)}, device_id_type=MESH,
         )
 
@@ -132,25 +136,34 @@
         rows = base + lax.broadcasted_iota(jnp.int32, (256, 2 * slots), 0)
         return jnp.where(rows == send_row[...], 1.0, 0.0).astype(BF16)
 
-    def pack_kv(base):
+    def pack_kv(g, base):
         chosen = pick(base)
-        for c in range(columns // 256):
-            pay_kv[pl.ds(base, 256), pl.ds(c * 256, 256)] = dot(
-                chosen, kv_stack[:, pl.ds(c * 256, 256)]
+        for c in range(span // 256):
+            pay_kv[g, pl.ds(base, 256), pl.ds(c * 256, 256)] = dot(
+                chosen, kv_stack[:, pl.ds(g * span + c * 256, 256)]
             ).astype(BF16)
 
     for load in loads[:2]:
         load.wait()
-    pack_kv(0)
+    pack_kv(0, 0)
     pl.semaphore_wait(barrier, n - 1)
     group = 256 // PAIR
-    start_range(kv_copy, 1, group)
+    kv_first = functools.partial(kv_copy, 0)
+    kv_second = functools.partial(kv_copy, 1)
+    start_range(kv_first, 1, group)
     for step in range(n):
         labels[step] = label[step : step + 1, :]
     start_range(label_copy, 1, n)
     for part in range(1, n // group):
-        pack_kv(part * 256)
-        start_range(kv_copy, part * group, (part + 1) * group)
+        pack_kv(0, part * 256)
+        start_range(kv_first, part * group, (part + 1) * group)
+
+    def pack_later(step, carry):
+        pack_kv(1, pl.multiple_of(step * 256, 256))
+        return carry
+
+    lax.fori_loop(0, n // group, pack_later, 0)
+    start_range(kv_second, 1, (3 * n) // 8)
 
     for load in loads[2:4]:
         load.wait()
@@ -165,7 +178,8 @@
         return carry
 
     lax.fori_loop(0, n // group, pack_q, 0)
-    got_kv[pl.ds(0, PAIR)] = pay_kv[pl.ds(0, PAIR)]
+    for g in range(GROUPS):
+        got_kv[g, pl.ds(0, PAIR)] = pay_kv[g, pl.ds(0, PAIR)]
     got_q[pl.ds(0, PAIR)] = pay_q[pl.ds(0, PAIR)]
     got_labels[0] = labels[0]
 
@@ -178,17 +192,17 @@
             device_id={"seq": lax.rem(me + 1, n)}, device_id_type=MESH,
         )
 
-    def all_kv():
-        return pltpu.make_async_remote_copy(
-            src_ref=pay_kv.at[rest], dst_ref=got_kv.at[rest],
+    def all_kv(g):
+        return pltpu.make_async_remote_copy(
+            src_ref=pay_kv.at[g, rest], dst_ref=got_kv.at[g, rest],
+            send_sem=send_sem.at[4 + g], recv_sem=recv_sem.at[4 + g],
+            device_id={"seq": lax.rem(me + 1, n)}, device_id_type=MESH,
+        )
+
+    def all_q():
+        return pltpu.make_async_remote_copy(
+            src_ref=pay_q.at[rest], dst_ref=got_q.at[rest],
             send_sem=send_sem.at[1], recv_sem=recv_sem.at[1],
-            device_id={"seq": lax.rem(me + 1, n)}, device_id_type=MESH,
-        )
-
-    def all_q():
-        return pltpu.make_async_remote_copy(
-            src_ref=pay_q.at[rest], dst_ref=got_q.at[rest],
-            send_sem=send_sem.at[2], recv_sem=recv_sem.at[2],
             device_id={"seq": lax.rem(me + 1, n)}, device_id_type=MESH,
         )
 
@@ -282,106 +296,102 @@
         rows = lax.broadcasted_iota(jnp.int32, (2 * slots, HD), 0)
         place[:, pl.ds(c * HD, HD)] = jnp.where(rows == piece, 1.0, 0.0).astype(BF16)
 
-    start_range(q_copy, 1, n // 4)
-
-    all_kv().wait_recv()
-
-    def arrange_kv(step, carry):
-        cols = pl.ds(pl.multiple_of(step * 256, 256), 256)
-        whole = dot(place[...], got_kv[:, cols]).astype(BF16)
-        k_all[pl.ds(resident, slots), cols] = whole[:slots]
-        v_all[pl.ds(resident, slots), cols] = whole[slots:]
-        return carry
-
-    lax.fori_loop(0, columns // 256, arrange_kv, 0)
-
-    def first_copy(step):
+    def arrange_kv(g):
+        def one(step, carry):
+            cols = pl.ds(pl.multiple_of(step * 256, 256), 256)
+            home = pl.ds(pl.multiple_of(g * span + step * 256, 256), 256)
+            whole = dot(place[...], got_kv[g, :, cols]).astype(BF16)
+            k_all[pl.ds(resident, slots), home] = whole[:slots]
+            v_all[pl.ds(resident, slots), home] = whole[slots:]
+            return carry
+
+        lax.fori_loop(0, span // 256, one, 0)
+
+    def first_copy(g, step):
         mate = lax.rem(p + step, plane)
         return pltpu.make_async_remote_copy(
-            src_ref=end.at[mate], dst_ref=in1.at[step],
-            send_sem=send_sem.at[3], recv_sem=recv_sem.at[3],
+            src_ref=end.at[g * plane + mate], dst_ref=in1.at[g * plane + step],
+            send_sem=send_sem.at[6 + g], recv_sem=recv_sem.at[6 + g],
             device_id={"seq": z * plane + mate}, device_id_type=MESH,
         )
 
-    def third_copy(step):
+    def third_copy(g, step):
         mate = lax.rem(p + step, plane)
         return pltpu.make_async_remote_copy(
-            src_ref=out3.at[mate], dst_ref=in3.at[step],
-            send_sem=send_sem.at[4], recv_sem=recv_sem.at[4],
+            src_ref=out3.at[g * plane + mate], dst_ref=in3.at[g * plane + step],
+            send_sem=send_sem.at[2 + g], recv_sem=recv_sem.at[2 + g],
             device_id={"seq": z * plane + mate}, device_id_type=MESH,
         )
 
-    def second_copy(step):
-        return pltpu.make_async_remote_copy(
-            src_ref=total, dst_ref=in2.at[step],
-            send_sem=send2.at[step], recv_sem=recv2.at[step],
+    def second_copy(g, step):
+        return pltpu.make_async_remote_copy(
+            src_ref=total.at[g], dst_ref=in2.at[g * depth + step],
+            send_sem=send2.at[g * depth + step], recv_sem=recv2.at[g * depth + step],
             device_id={"seq": lax.rem(me + step * plane, n)}, device_id_type=MESH,
         )
 
-    def all_first():
-        return pltpu.make_async_remote_copy(
-            src_ref=end.at[pl.ds(1, plane - 1)], dst_ref=in1.at[pl.ds(1, plane - 1)],
-            send_sem=send_sem.at[3], recv_sem=recv_sem.at[3],
+    def all_first(g):
+        pieces = pl.ds(g * plane + 1, plane - 1)
+        return pltpu.make_async_remote_copy(
+            src_ref=end.at[pieces], dst_ref=in1.at[pieces],
+            send_sem=send_sem.at[6 + g], recv_sem=recv_sem.at[6 + g],
             device_id={"seq": z * plane + lax.rem(p + 1, plane)}, device_id_type=MESH,
         )
 
-    def all_third():
-        return pltpu.make_async_remote_copy(
-            src_ref=out3.at[pl.ds(1, plane - 1)], dst_ref=in3.at[pl.ds(1, plane - 1)],
-            send_sem=send_sem.at[4], recv_sem=recv_sem.at[4],
+    def all_third(g):
+        pieces = pl.ds(g * plane + 1, plane - 1)
+        return pltpu.make_async_remote_copy(
+            src_ref=out3.at[pieces], dst_ref=in3.at[pieces],
+            send_sem=send_sem.at[2 + g], recv_sem=recv_sem.at[2 + g],
             device_id={"seq": z * plane + lax.rem(p + 1, plane)}, device_id_type=MESH,
         )
 
-    def end_head(h):
-        end[h] = step_state(last, h, rate_ref[h], s_local[last, h])
-
-    def end_mate(step, carry):
-        end_head(lax.rem(p + step, plane))
-        first_copy(step).start()
-        return carry
-
-    lax.fori_loop(1, plane, end_mate, 0)
-    start_range(q_copy, n // 4, n // 2)
-    end_head(p)
-    in1[0] = end[p]
-    rate_p = rate_ref[p]
-    all_first().wait_recv()
-
-    state = jnp.zeros((HD, HD), F32)
-    for m in range(plane):
-        shard = z * plane + m
-        out3[m] = state
-        pass_on = decay_of(-rate_p * length) * clear(shard * length, (shard + 1) * length)
-        state = pass_on * state + in1[lax.rem(p - m + plane, plane)]
-    total[...] = state.astype(BF16)
-
-    for step in range(1, depth):
-        @pl.when(z + step < depth)
-        def _(step=step):
-            second_copy(step).start()
-
-    start_range(q_copy, n // 2, (3 * n) // 4)
-
-    before[...] = jnp.zeros((HD, HD), F32)
-    span = plane * length
-    for step in range(1, depth):
-        @pl.when(z - step >= 0)
-        def _(step=step):
-            second_copy(step).wait_recv()
-            factor = decay_of(-rate_p * float(span * (step - 1))) * clear(
-                (z - step + 1) * span, z * span
+    plane_rows = plane * length
+
+    def ends(g):
+        def one(i, carry):
+            h = g * heads_in + i
+            state = step_state(last, h, rate_ref[h], s_local[last, h])
+            for m in range(GROUPS):
+                end[h * GROUPS + m] = state[m * piece_rows : (m + 1) * piece_rows]
+            return carry
+
+        lax.fori_loop(0, heads_in, one, 0, unroll=2)
+        start_range(functools.partial(first_copy, g), 1, plane)
+        in1[g * plane] = end[g * plane + p]
+
+    def totals(g, rate_p):
+        all_first(g).wait_recv()
+        state = jnp.zeros((piece_rows, HD), F32)
+        for m in range(plane):
+            shard = z * plane + m
+            out3[g * plane + m] = state
+            pass_on = decay_of(-rate_p * length) * clear(shard * length, (shard + 1) * length)
+            state = pass_on * state + in1[g * plane + lax.rem(p - m + plane, plane)]
+        total[g] = state.astype(BF16)
+        for step in range(1, depth):
+            @pl.when(z + step < depth)
+            def _(step=step):
+                second_copy(g, step).start()
+
+    def prefixes(g, rate_p):
+        before[...] = jnp.zeros((piece_rows, HD), F32)
+        for step in range(1, depth):
+            @pl.when(z - step >= 0)
+            def _(step=step):
+                second_copy(g, step).wait_recv()
+                factor = decay_of(-rate_p * float(plane_rows * (step - 1))) * clear(
+                    (z - step + 1) * plane_rows, z * plane_rows
+                )
+                before[...] = before[...] + factor * in2[g * depth + step].astype(F32)
+        earlier = before[...]
+        for m in range(plane):
+            factor = decay_of(-rate_p * float(length * m)) * clear(
+                z * plane_rows, z * plane_rows + m * length
             )
-            before[...] = before[...] + factor * in2[step].astype(F32)
-
-    earlier = before[...]
-    for m in range(plane):
-        factor = decay_of(-rate_p * float(length * m)) * clear(z * span, z * span + m * length)
-        out3[m] = out3[m] + factor * earlier
-
-    start_range(third_copy, 1, plane)
-    start_range(q_copy, (3 * n) // 4, n)
-    in3[0] = out3[p]
-    all_third().wait_recv()
+            out3[g * plane + m] = out3[g * plane + m] + factor * earlier
+        start_range(functools.partial(third_copy, g), 1, plane)
+        in3[g * plane] = out3[g * plane + p]
 
     def finish(c, h, rate, local):
         rows = pl.ds(c * CHUNK, CHUNK)
@@ -389,7 +399,12 @@
         reach = decay_of(-rate * float(c * CHUNK))
         for m in range(c):
             reach = reach * alive[m, CHUNK - 1 : CHUNK, :]
-        carry = s_local[c, h] + reach * in3[lax.rem(p - h + plane, plane)]
+        g = h // heads_in
+        owner = (h - g * heads_in) * GROUPS
+        carried = jnp.concatenate(
+            [in3[g * plane + lax.rem(p - owner - m + plane, plane)] for m in range(GROUPS)], axis=0
+        )
+        carry = s_local[c, h] + reach * carried
         spot = lax.broadcasted_iota(jnp.int32, (CHUNK, HD), 0).astype(F32)
         into = jnp.exp(-rate * (spot + 1.0)) * alive[c]
         whole = local + into * fold(dot(q_all[rows, cols], two_terms(carry)))
@@ -403,7 +418,32 @@
             finish(c, h, rate, o_local[pl.ds(c * CHUNK, CHUNK), cols])
         return carry
 
-    lax.fori_loop(0, plane, finish_resident, 0, unroll=2)
+    def finish_group(g):
+        all_third(g).wait_recv()
+        lax.fori_loop(g * heads_in, (g + 1) * heads_in, finish_resident, 0, unroll=2)
+
+    rates = [rate_ref[g * heads_in + p // GROUPS] for g in range(GROUPS)]
+
+    all_kv(0).wait_recv()
+    arrange_kv(0)
+    ends(0)
+    start_range(kv_second, (3 * n) // 8, (5 * n) // 8)
+    totals(0, rates[0])
+    start_range(kv_second, (5 * n) // 8, (13 * n) // 16)
+    prefixes(0, rates[0])
+    start_range(kv_second, (13 * n) // 16, n)
+    start_range(q_copy, 1, n // 4)
+
+    all_kv(1).wait_recv()
+    arrange_kv(1)
+    ends(1)
+    start_range(q_copy, n // 4, n // 2)
+    finish_group(0)
+    totals(1, rates[1])
+    start_range(q_copy, n // 2, (3 * n) // 4)
+    prefixes(1, rates[1])
+    start_range(q_copy, (3 * n) // 4, n)
+    finish_group(1)
     rows_in = pl.ds(0, resident)
     rows_new = pl.ds(resident, slots)
     store = pltpu.make_async_copy(done.at[rows_in], out.at[rows_in], out_sem.at[0])
@@ -431,14 +471,15 @@
     store_new.start()
 
     all_labels().wait_send()
-    all_kv().wait_send()
     all_q().wait_send()
-    all_first().wait_send()
-    all_third().wait_send()
-    for step in range(1, depth):
-        @pl.when(z + step < depth)
-        def _(step=step):
-            second_copy(step).wait_send()
+    for g in range(GROUPS):
+        all_kv(g).wait_send()
+        all_first(g).wait_send()
+        all_third(g).wait_send()
+        for step in range(1, depth):
+            @pl.when(z + step < depth)
+            def _(g=g, step=step):
+                second_copy(g, step).wait_send()
     store.wait()
     store_new.wait()
 
@@ -488,9 +529,9 @@
             pltpu.VMEM((length, columns), BF16),
             pltpu.VMEM((2 * fresh, columns), BF16),
             pltpu.VMEM((2 * fresh, columns // 2), BF16),
-            pltpu.VMEM((n * PAIR, columns), BF16),
+            pltpu.VMEM((GROUPS, n * PAIR, columns // GROUPS), BF16),
             pltpu.VMEM((n * PAIR, columns // 2), BF16),
-            pltpu.VMEM((n * PAIR, columns), BF16),
+            pltpu.VMEM((GROUPS, n * PAIR, columns // GROUPS), BF16),
             pltpu.VMEM((n * PAIR, columns // 2), BF16),
             pltpu.VMEM((n, 1, HD), jnp.int32),
             pltpu.VMEM((2 * fresh, n * PAIR), BF16),
@@ -499,19 +540,19 @@
             pltpu.VMEM((chunks, CHUNK, HD), F32),
             pltpu.VMEM((resident, columns), F32),
             pltpu.VMEM((chunks, heads, HD, HD), F32),
-            pltpu.VMEM((heads, HD, HD), F32),
-            pltpu.VMEM((heads, HD, HD), F32),
-            pltpu.VMEM((HD, HD), BF16),
-            pltpu.VMEM((n // heads, HD, HD), BF16),
-            pltpu.VMEM((HD, HD), F32),
-            pltpu.VMEM((heads, HD, HD), F32),
-            pltpu.VMEM((heads, HD, HD), F32),
+            pltpu.VMEM((GROUPS * heads, HD // GROUPS, HD), F32),
+            pltpu.VMEM((GROUPS * heads, HD // GROUPS, HD), F32),
+            pltpu.VMEM((GROUPS, HD // GROUPS, HD), BF16),
+            pltpu.VMEM((GROUPS * (n // heads), HD // GROUPS, HD), BF16),
+            pltpu.VMEM((HD // GROUPS, HD), F32),
+            pltpu.VMEM((GROUPS * heads, HD // GROUPS, HD), F32),
+            pltpu.VMEM((GROUPS * heads, HD // GROUPS, HD), F32),
             pltpu.VMEM((length, columns), BF16),
             pltpu.SemaphoreType.DMA((7,)),
-            pltpu.SemaphoreType.DMA((5,)),
-            pltpu.SemaphoreType.DMA((5,)),
-            pltpu.SemaphoreType.DMA((n // heads,)),
-            pltpu.SemaphoreType.DMA((n // heads,)),
+            pltpu.SemaphoreType.DMA((4 + 2 * GROUPS,)),
+            pltpu.SemaphoreType.DMA((4 + 2 * GROUPS,)),
+            pltpu.SemaphoreType.DMA((GROUPS * (n // heads),)),
+            pltpu.SemaphoreType.DMA((GROUPS * (n // heads),)),
             pltpu.SemaphoreType.DMA((2,)),
         ],
         compiler_params=pltpu.CompilerParams(

time: 100 us -> 97.1 us (0.971)
  Pallas kernels: 99.6 us -> 96.9 us
    pallas_call x1, Pallas kernels: 97.2 us -> 94.5 us  [body(): pl.pallas_call(functools.partial(kernel, n, heads), out_shape=jax.ShapeDt...]
where the time goes in v4:
time: 97.1 us; the launch traced here: 96.9 us
  Pallas kernels  96.9 us (100%)
    pallas_call x1, Pallas kernels, body(): pl.pallas_call(functools.partial(kernel, n, heads), out_shape=jax.ShapeDt...  94.5 us
    pallas_call x1, Pallas kernels, body(): pl.pallas_call(functools.partial(hand_over, parts), out_shape=jax.ShapeDt...  2.39 us

profile of v4, /device:TPU:1, one launch (start us, length us, event | category | flops | bytes accessed | tf_op | source)
XLA Modules:
  0.0 96.9 jit_solution(3490624967185356464)
XLA Ops:
  0.0 94.5 %shard_map.100.src = bf16[1024,1024]{1,0:T(8,128)(2,1)} custom-call(bf16[768,1024]{1,0:T(8,128)(2,1)} %q_res.1, bf16[768,1024]{1,0:T(8,128)(2,1)} %k_res.1, bf16[768,1024]{1,0:T(8,128)(2,1)} %v_res.1, bf16[256,1024]{1,0:T(8,128)(2,1)} %q_new.1, bf16[256,1024]{1,0:T(8,128)(2,1)} %k_new.1, bf16[256,1024]{1,0:T(8,128)(2,1)} %v_new.1, s32[32]{0:T(128)} %dest_ref.1, ...), custom_call_target="tpu_custom_call" | custom-call | tf_op jit(solution)/shard_map/pallas_call | solution.py:517
  94.5 2.4 %shard_map.101 = bf16[1024,1024]{1,0:T(8,128)(2,1)} custom-call(bf16[1024,1024]{1,0:T(8,128)(2,1)} %shard_map.100.src), custom_call_target="tpu_custom_call" | custom-call | tf_op jit(solution)/shard_map/pallas_call | solution.py:563

commit v5 on v4

--- a/solution.py
+++ b/solution.py
@@ -45,8 +45,8 @@
     n, plane, q_res, k_res, v_res, q_new, k_new, v_new, dest_ref, slot_ref, bound_ref, rate_ref, out,
     send_row, labels, b_row, b_col,
     q_all, k_all, v_all, kv_stack, q_stack, pay_kv, pay_q, got_kv, got_q, got_labels, place,
-    mask, alive, keep, o_local, s_local, end, in1, total, in2, before, out3, in3, done,
-    load_sem, send_sem, recv_sem, send2, recv2, out_sem,
+    mask, alive, keep, o_local, s_local, end, in1, total, in2, before, out3, in3, done, relay,
+    load_sem, send_sem, recv_sem, send2, recv2, out_sem, relay_recv, pass_send,
 ):
     me = lax.axis_index("seq")
     z, p = me // plane, lax.rem(me, plane)
@@ -132,6 +132,79 @@
 
         lax.fori_loop(low, high, one, 0)
 
+    hop = depth // 4
+
+    def is_far(step):
+        return lax.rem(ahead(step) // plane - z + depth, depth) == depth // 2
+
+    def payload(k):
+        return pay_q if k == GROUPS else pay_kv.at[k]
+
+    def arrived(k):
+        return got_q if k == GROUPS else got_kv.at[k]
+
+    def payload_sem(k):
+        return 1 if k == GROUPS else 4 + k
+
+    def direct_copy(k, step):
+        return q_copy(step) if k == GROUPS else kv_copy(k, step)
+
+    def relay_copy(k, step):
+        place_in = lax.rem(ahead(step), plane)
+        way = 1 - 2 * lax.rem(place_in, 2)
+        return pltpu.make_async_remote_copy(
+            src_ref=payload(k).at[pl.ds(pl.multiple_of(step * PAIR, PAIR), PAIR)],
+            dst_ref=relay.at[k, pl.ds(pl.multiple_of(place_in * PAIR, PAIR), PAIR)],
+            send_sem=send_sem.at[payload_sem(k)], recv_sem=relay_recv.at[k],
+            device_id={"seq": lax.rem(me + way * hop * plane + n, n)}, device_id_type=MESH,
+        )
+
+    def pass_copy(k, place_in):
+        way = 1 - 2 * lax.rem(place_in, 2)
+        source = lax.rem(me - way * hop * plane + n, n)
+        target = lax.rem(z + way * hop + depth, depth) * plane + place_in
+        slot = lax.rem((target - source) * side * back + n * n, n)
+        return pltpu.make_async_remote_copy(
+            src_ref=relay.at[k, pl.ds(pl.multiple_of(place_in * PAIR, PAIR), PAIR)],
+            dst_ref=arrived(k).at[pl.ds(pl.multiple_of(slot * PAIR, PAIR), PAIR)],
+            send_sem=pass_send.at[k], recv_sem=recv_sem.at[payload_sem(k)],
+            device_id={"seq": target}, device_id_type=MESH,
+        )
+
+    def relayed(k):
+        return pltpu.make_async_remote_copy(
+            src_ref=relay.at[k], dst_ref=relay.at[k],
+            send_sem=pass_send.at[k], recv_sem=relay_recv.at[k],
+            device_id={"seq": lax.rem(me + 1, n)}, device_id_type=MESH,
+        )
+
+    def start_far(k, low, high):
+        def one(step, carry):
+            @pl.when(is_far(step))
+            def _():
+                relay_copy(k, step).start()
+            return carry
+
+        lax.fori_loop(low, high, one, 0)
+
+    def start_near(k, low, high):
+        def one(step, carry):
+            @pl.when(jnp.logical_not(is_far(step)))
+            def _():
+                direct_copy(k, step).start()
+            return carry
+
+        lax.fori_loop(low, high, one, 0)
+
+    def pass_on_all(k):
+        relayed(k).wait_recv()
+
+        def one(place_in, carry):
+            pass_copy(k, place_in).start()
+            return carry
+
+        lax.fori_loop(0, plane, one, 0)
+
     def pick(base):
         rows = base + lax.broadcasted_iota(jnp.int32, (256, 2 * slots), 0)
         return jnp.where(rows == send_row[...], 1.0, 0.0).astype(BF16)
@@ -148,22 +221,22 @@
     pack_kv(0, 0)
     pl.semaphore_wait(barrier, n - 1)
     group = 256 // PAIR
-    kv_first = functools.partial(kv_copy, 0)
-    kv_second = functools.partial(kv_copy, 1)
-    start_range(kv_first, 1, group)
+    start_far(0, 1, group)
+    start_near(0, 1, group)
     for step in range(n):
         labels[step] = label[step : step + 1, :]
     start_range(label_copy, 1, n)
     for part in range(1, n // group):
         pack_kv(0, part * 256)
-        start_range(kv_first, part * group, (part + 1) * group)
+    start_far(0, group, n)
+    start_near(0, group, n)
 
     def pack_later(step, carry):
         pack_kv(1, pl.multiple_of(step * 256, 256))
         return carry
 
     lax.fori_loop(0, n // group, pack_later, 0)
-    start_range(kv_second, 1, (3 * n) // 8)
+    start_far(1, 1, n)
 
     for load in loads[2:4]:
         load.wait()
@@ -280,7 +353,10 @@
         s_local[last, h] = state
         return carry
 
-    lax.fori_loop(0, plane, resident_head, 0)
+    lax.fori_loop(0, heads_in, resident_head, 0)
+    pass_on_all(0)
+    start_near(1, 1, (3 * n) // 8)
+    lax.fori_loop(heads_in, plane, resident_head, 0)
 
     all_labels().wait_recv()
     lane = lax.broadcasted_iota(jnp.int32, (1, HD), 1)
@@ -427,22 +503,25 @@
     all_kv(0).wait_recv()
     arrange_kv(0)
     ends(0)
-    start_range(kv_second, (3 * n) // 8, (5 * n) // 8)
+    start_near(1, (3 * n) // 8, (5 * n) // 8)
     totals(0, rates[0])
-    start_range(kv_second, (5 * n) // 8, (13 * n) // 16)
+    pass_on_all(1)
+    start_near(1, (5 * n) // 8, (13 * n) // 16)
     prefixes(0, rates[0])
-    start_range(kv_second, (13 * n) // 16, n)
-    start_range(q_copy, 1, n // 4)
+    start_near(1, (13 * n) // 16, n)
+    start_far(2, 1, n)
+    start_near(2, 1, n // 4)
 
     all_kv(1).wait_recv()
     arrange_kv(1)
     ends(1)
-    start_range(q_copy, n // 4, n // 2)
+    start_near(2, n // 4, n // 2)
     finish_group(0)
     totals(1, rates[1])
-    start_range(q_copy, n // 2, (3 * n) // 4)
+    pass_on_all(2)
+    start_near(2, n // 2, (3 * n) // 4)
     prefixes(1, rates[1])
-    start_range(q_copy, (3 * n) // 4, n)
+    start_near(2, (3 * n) // 4, n)
     finish_group(1)
     rows_in = pl.ds(0, resident)
     rows_new = pl.ds(resident, slots)
@@ -472,6 +551,8 @@
 
     all_labels().wait_send()
     all_q().wait_send()
+    for k in range(GROUPS + 1):
+        relayed(k).wait_send()
     for g in range(GROUPS):
         all_kv(g).wait_send()
         all_first(g).wait_send()
@@ -548,12 +629,15 @@
             pltpu.VMEM((GROUPS * heads, HD // GROUPS, HD), F32),
             pltpu.VMEM((GROUPS * heads, HD // GROUPS, HD), F32),
             pltpu.VMEM((length, columns), BF16),
+            pltpu.VMEM((GROUPS + 1, heads * PAIR, columns // GROUPS), BF16),
             pltpu.SemaphoreType.DMA((7,)),
             pltpu.SemaphoreType.DMA((4 + 2 * GROUPS,)),
             pltpu.SemaphoreType.DMA((4 + 2 * GROUPS,)),
             pltpu.SemaphoreType.DMA((GROUPS * (n // heads),)),
             pltpu.SemaphoreType.DMA((GROUPS * (n // heads),)),
             pltpu.SemaphoreType.DMA((2,)),
+            pltpu.SemaphoreType.DMA((GROUPS + 1,)),
+            pltpu.SemaphoreType.DMA((GROUPS + 1,)),
         ],
         compiler_params=pltpu.CompilerParams(
             collective_id=0, has_side_effects=True, vmem_limit_bytes=60 * 1024 * 1024

time: 97.1 us -> 99.9 us (1.029)
  Pallas kernels: 96.9 us -> 99.7 us
    pallas_call x1, Pallas kernels: 94.5 us -> 97.3 us  [body(): pl.pallas_call(functools.partial(kernel, n, heads), out_shape=jax.ShapeDt...]
where the time goes in v5:
time: 99.9 us; the launch traced here: 99.8 us
  Pallas kernels  99.7 us (100%)
    pallas_call x1, Pallas kernels, body(): pl.pallas_call(functools.partial(kernel, n, heads), out_shape=jax.ShapeDt...  97.3 us
    pallas_call x1, Pallas kernels, body(): pl.pallas_call(functools.partial(hand_over, parts), out_shape=jax.ShapeDt...  2.39 us

profile of v5, /device:TPU:1, one launch (start us, length us, event | category | flops | bytes accessed | tf_op | source)
XLA Modules:
  0.0 99.8 jit_solution(12553650129298723064)
XLA Ops:
  0.0 97.3 %shard_map.100.src = bf16[1024,1024]{1,0:T(8,128)(2,1)} custom-call(bf16[768,1024]{1,0:T(8,128)(2,1)} %q_res.1, bf16[768,1024]{1,0:T(8,128)(2,1)} %k_res.1, bf16[768,1024]{1,0:T(8,128)(2,1)} %v_res.1, bf16[256,1024]{1,0:T(8,128)(2,1)} %q_new.1, bf16[256,1024]{1,0:T(8,128)(2,1)} %k_new.1, bf16[256,1024]{1,0:T(8,128)(2,1)} %v_new.1, s32[32]{0:T(128)} %dest_ref.1, ...), custom_call_target="tpu_custom_call" | custom-call | tf_op jit(solution)/shard_map/pallas_call | solution.py:598
  97.4 2.4 %shard_map.101 = bf16[1024,1024]{1,0:T(8,128)(2,1)} custom-call(bf16[1024,1024]{1,0:T(8,128)(2,1)} %shard_map.100.src), custom_call_target="tpu_custom_call" | custom-call | tf_op jit(solution)/shard_map/pallas_call | solution.py:647

commit v6 on v4

--- a/solution.py
+++ b/solution.py
@@ -57,21 +57,28 @@
     last = chunks - 1
     slots = CHUNK
     columns = q_res.shape[1]
-    half = columns // 2
     span = columns // GROUPS
+    half = span // 2
     heads_in = plane // GROUPS
     piece_rows = HD // GROUPS
 
     loads = [
         pltpu.make_async_copy(k_new, kv_stack.at[pl.ds(0, slots)], load_sem.at[0]),
         pltpu.make_async_copy(v_new, kv_stack.at[pl.ds(slots, slots)], load_sem.at[1]),
-        pltpu.make_async_copy(q_new.at[:, pl.ds(0, half)], q_stack.at[pl.ds(0, slots)], load_sem.at[2]),
-        pltpu.make_async_copy(q_new.at[:, pl.ds(half, half)], q_stack.at[pl.ds(slots, slots)], load_sem.at[3]),
-        pltpu.make_async_copy(q_res, q_all.at[pl.ds(0, resident)], load_sem.at[4]),
-        pltpu.make_async_copy(k_res, k_all.at[pl.ds(0, resident)], load_sem.at[5]),
-        pltpu.make_async_copy(v_res, v_all.at[pl.ds(0, resident)], load_sem.at[6]),
+        pltpu.make_async_copy(q_res, q_all.at[pl.ds(0, resident)], load_sem.at[2]),
+        pltpu.make_async_copy(k_res, k_all.at[pl.ds(0, resident)], load_sem.at[3]),
+        pltpu.make_async_copy(v_res, v_all.at[pl.ds(0, resident)], load_sem.at[4]),
     ]
-    for load in loads:
+    q_loads = [
+        pltpu.make_async_copy(
+            q_new.at[:, pl.ds(g * span + m * half, half)],
+            q_stack.at[g, pl.ds(m * slots, slots)],
+            load_sem.at[5 + 2 * g + m],
+        )
+        for g in range(GROUPS)
+        for m in range(2)
+    ]
+    for load in loads[:2] + q_loads + loads[2:]:
         load.start()
 
     barrier = pltpu.get_barrier_semaphore()
@@ -117,11 +124,11 @@
             device_id={"seq": ahead(step)}, device_id_type=MESH,
         )
 
-    def q_copy(step):
+    def q_copy(g, step):
         rows = pl.ds(pl.multiple_of(step * PAIR, PAIR), PAIR)
         return pltpu.make_async_remote_copy(
-            src_ref=pay_q.at[rows], dst_ref=got_q.at[rows],
-            send_sem=send_sem.at[1], recv_sem=recv_sem.at[1],
+            src_ref=pay_q.at[g, rows], dst_ref=got_q.at[g, rows],
+            send_sem=send_sem.at[8 + g], recv_sem=recv_sem.at[8 + g],
             device_id={"seq": ahead(step)}, device_id_type=MESH,
         )
 
@@ -165,22 +172,20 @@
     lax.fori_loop(0, n // group, pack_later, 0)
     start_range(kv_second, 1, (3 * n) // 8)
 
-    for load in loads[2:4]:
+    for load in q_loads:
         load.wait()
 
     def pack_q(step, carry):
         base = pl.multiple_of(step * 256, 256)
         chosen = pick(base)
-        for c in range(half // 256):
-            pay_q[pl.ds(base, 256), pl.ds(c * 256, 256)] = dot(
-                chosen, q_stack[:, pl.ds(c * 256, 256)]
-            ).astype(BF16)
+        for g in range(GROUPS):
+            pay_q[g, pl.ds(base, 256)] = dot(chosen, q_stack[g]).astype(BF16)
         return carry
 
     lax.fori_loop(0, n // group, pack_q, 0)
     for g in range(GROUPS):
         got_kv[g, pl.ds(0, PAIR)] = pay_kv[g, pl.ds(0, PAIR)]
-    got_q[pl.ds(0, PAIR)] = pay_q[pl.ds(0, PAIR)]
+        got_q[g, pl.ds(0, PAIR)] = pay_q[g, pl.ds(0, PAIR)]
     got_labels[0] = labels[0]
 
     rest = pl.ds(PAIR, (n - 1) * PAIR)
@@ -199,10 +204,10 @@
             device_id={"seq": lax.rem(me + 1, n)}, device_id_type=MESH,
         )
 
-    def all_q():
-        return pltpu.make_async_remote_copy(
-            src_ref=pay_q.at[rest], dst_ref=got_q.at[rest],
-            send_sem=send_sem.at[1], recv_sem=recv_sem.at[1],
+    def all_q(g):
+        return pltpu.make_async_remote_copy(
+            src_ref=pay_q.at[g, rest], dst_ref=got_q.at[g, rest],
+            send_sem=send_sem.at[8 + g], recv_sem=recv_sem.at[8 + g],
             device_id={"seq": lax.rem(me + 1, n)}, device_id_type=MESH,
         )
 
@@ -265,7 +270,7 @@
         weights = (scores * (decay * mask[c])).astype(BF16)
         return dot(weights, v_all[rows, cols])
 
-    for load in loads[4:]:
+    for load in loads[2:]:
         load.wait()
 
     def resident_head(h, carry):
@@ -422,7 +427,22 @@
         all_third(g).wait_recv()
         lax.fori_loop(g * heads_in, (g + 1) * heads_in, finish_resident, 0, unroll=2)
 
+    def finish_admitted(h, carry):
+        rate = rate_ref[h]
+        finish(last, h, rate, local_part(last, h, decay_matrix(rate)))
+        return carry
+
+    def finish_new(g):
+        all_q(g).wait_recv()
+        whole = dot(place[...], got_q[g]).astype(BF16)
+        for m in range(2):
+            home = pl.ds(g * span + m * half, half)
+            q_all[pl.ds(resident, slots), home] = whole[m * slots : (m + 1) * slots]
+        lax.fori_loop(g * heads_in, (g + 1) * heads_in, finish_admitted, 0, unroll=4)
+
     rates = [rate_ref[g * heads_in + p // GROUPS] for g in range(GROUPS)]
+    q_first = functools.partial(q_copy, 0)
+    q_second = functools.partial(q_copy, 1)
 
     all_kv(0).wait_recv()
     arrange_kv(0)
@@ -432,48 +452,31 @@
     start_range(kv_second, (5 * n) // 8, (13 * n) // 16)
     prefixes(0, rates[0])
     start_range(kv_second, (13 * n) // 16, n)
-    start_range(q_copy, 1, n // 4)
+    start_range(q_first, 1, n // 2)
 
     all_kv(1).wait_recv()
     arrange_kv(1)
     ends(1)
-    start_range(q_copy, n // 4, n // 2)
+    start_range(q_first, n // 2, n)
     finish_group(0)
     totals(1, rates[1])
-    start_range(q_copy, n // 2, (3 * n) // 4)
+    start_range(q_second, 1, n // 2)
     prefixes(1, rates[1])
-    start_range(q_copy, (3 * n) // 4, n)
+    start_range(q_second, n // 2, n)
+    finish_new(0)
     finish_group(1)
     rows_in = pl.ds(0, resident)
     rows_new = pl.ds(resident, slots)
     store = pltpu.make_async_copy(done.at[rows_in], out.at[rows_in], out_sem.at[0])
     store.start()
-
-    all_q().wait_recv()
-
-    def arrange_q(step, carry):
-        cols = pl.ds(pl.multiple_of(step * 256, 256), 256)
-        later = pl.ds(pl.multiple_of(half + step * 256, 256), 256)
-        whole = dot(place[...], got_q[:, cols]).astype(BF16)
-        q_all[pl.ds(resident, slots), cols] = whole[:slots]
-        q_all[pl.ds(resident, slots), later] = whole[slots:]
-        return carry
-
-    lax.fori_loop(0, half // 256, arrange_q, 0)
-
-    def finish_admitted(h, carry):
-        rate = rate_ref[h]
-        finish(last, h, rate, local_part(last, h, decay_matrix(rate)))
-        return carry
-
-    lax.fori_loop(0, plane, finish_admitted, 0, unroll=2)
+    finish_new(1)
     store_new = pltpu.make_async_copy(done.at[rows_new], out.at[rows_new], out_sem.at[1])
     store_new.start()
 
     all_labels().wait_send()
-    all_q().wait_send()
     for g in range(GROUPS):
         all_kv(g).wait_send()
+        all_q(g).wait_send()
         all_first(g).wait_send()
         all_third(g).wait_send()
         for step in range(1, depth):
@@ -528,11 +531,11 @@
             pltpu.VMEM((length, columns), BF16),
             pltpu.VMEM((length, columns), BF16),
             pltpu.VMEM((2 * fresh, columns), BF16),
-            pltpu.VMEM((2 * fresh, columns // 2), BF16),
+            pltpu.VMEM((GROUPS, 2 * fresh, columns // (2 * GROUPS)), BF16),
             pltpu.VMEM((GROUPS, n * PAIR, columns // GROUPS), BF16),
-            pltpu.VMEM((n * PAIR, columns // 2), BF16),
+            pltpu.VMEM((GROUPS, n * PAIR, columns // (2 * GROUPS)), BF16),
             pltpu.VMEM((GROUPS, n * PAIR, columns // GROUPS), BF16),
-            pltpu.VMEM((n * PAIR, columns // 2), BF16),
+            pltpu.VMEM((GROUPS, n * PAIR, columns // (2 * GROUPS)), BF16),
             pltpu.VMEM((n, 1, HD), jnp.int32),
             pltpu.VMEM((2 * fresh, n * PAIR), BF16),
             pltpu.VMEM((chunks, CHUNK, CHUNK), F32),
@@ -548,9 +551,9 @@
             pltpu.VMEM((GROUPS * heads, HD // GROUPS, HD), F32),
             pltpu.VMEM((GROUPS * heads, HD // GROUPS, HD), F32),
             pltpu.VMEM((length, columns), BF16),
-            pltpu.SemaphoreType.DMA((7,)),
-            pltpu.SemaphoreType.DMA((4 + 2 * GROUPS,)),
-            pltpu.SemaphoreType.DMA((4 + 2 * GROUPS,)),
+            pltpu.SemaphoreType.DMA((5 + 2 * GROUPS,)),
+            pltpu.SemaphoreType.DMA((4 + 3 * GROUPS,)),
+            pltpu.SemaphoreType.DMA((4 + 3 * GROUPS,)),
             pltpu.SemaphoreType.DMA((GROUPS * (n // heads),)),
             pltpu.SemaphoreType.DMA((GROUPS * (n // heads),)),
             pltpu.SemaphoreType.DMA((2,)),

time: 97.1 us -> 95.3 us (0.981)
  Pallas kernels: 96.9 us -> 95.1 us
    pallas_call x1, Pallas kernels: 94.5 us -> 92.7 us  [body(): pl.pallas_call(functools.partial(kernel, n, heads), out_shape=jax.ShapeDt...]
where the time goes in v6:
time: 95.3 us; the launch traced here: 95.1 us
  Pallas kernels  95.1 us (100%)
    pallas_call x1, Pallas kernels, body(): pl.pallas_call(functools.partial(kernel, n, heads), out_shape=jax.ShapeDt...  92.7 us
    pallas_call x1, Pallas kernels, body(): pl.pallas_call(functools.partial(hand_over, parts), out_shape=jax.ShapeDt...  2.39 us

profile of v6, /device:TPU:1, one launch (start us, length us, event | category | flops | bytes accessed | tf_op | source)
XLA Modules:
  0.0 95.1 jit_solution(11443029785310720787)
XLA Ops:
  0.0 92.7 %shard_map.100.src = bf16[1024,1024]{1,0:T(8,128)(2,1)} custom-call(bf16[768,1024]{1,0:T(8,128)(2,1)} %q_res.1, bf16[768,1024]{1,0:T(8,128)(2,1)} %k_res.1, bf16[768,1024]{1,0:T(8,128)(2,1)} %v_res.1, bf16[256,1024]{1,0:T(8,128)(2,1)} %q_new.1, bf16[256,1024]{1,0:T(8,128)(2,1)} %k_new.1, bf16[256,1024]{1,0:T(8,128)(2,1)} %v_new.1, s32[32]{0:T(128)} %dest_ref.1, ...), custom_call_target="tpu_custom_call" | custom-call | tf_op jit(solution)/shard_map/pallas_call | solution.py:520
  92.7 2.4 %shard_map.101 = bf16[1024,1024]{1,0:T(8,128)(2,1)} custom-call(bf16[1024,1024]{1,0:T(8,128)(2,1)} %shard_map.100.src), custom_call_target="tpu_custom_call" | custom-call | tf_op jit(solution)/shard_map/pallas_call | solution.py:566

commit v7 on v6

--- a/solution.py
+++ b/solution.py
@@ -62,6 +62,16 @@
     heads_in = plane // GROUPS
     piece_rows = HD // GROUPS
 
+    barrier = pltpu.get_barrier_semaphore()
+
+    def greet(step, carry):
+        pl.semaphore_signal(
+            barrier, inc=1, device_id={"seq": lax.rem(me + step, n)}, device_id_type=MESH
+        )
+        return carry
+
+    lax.fori_loop(1, n, greet, 0, unroll=7)
+
     loads = [
         pltpu.make_async_copy(k_new, kv_stack.at[pl.ds(0, slots)], load_sem.at[0]),
         pltpu.make_async_copy(v_new, kv_stack.at[pl.ds(slots, slots)], load_sem.at[1]),
@@ -80,16 +90,6 @@
     ]
     for load in loads[:2] + q_loads + loads[2:]:
         load.start()
-
-    barrier = pltpu.get_barrier_semaphore()
-
-    def greet(step, carry):
-        pl.semaphore_signal(
-            barrier, inc=1, device_id={"seq": lax.rem(me + step, n)}, device_id_type=MESH
-        )
-        return carry
-
-    lax.fori_loop(1, n, greet, 0)
 
     side = 1 - 2 * lax.rem(me, 2)
 
@@ -170,7 +170,7 @@
         return carry
 
     lax.fori_loop(0, n // group, pack_later, 0)
-    start_range(kv_second, 1, (3 * n) // 8)
+    start_range(kv_second, 1, (3 * n) // 4)
 
     for load in q_loads:
         load.wait()
@@ -285,7 +285,7 @@
         s_local[last, h] = state
         return carry
 
-    lax.fori_loop(0, plane, resident_head, 0)
+    lax.fori_loop(0, plane, resident_head, 0, unroll=2)
 
     all_labels().wait_recv()
     lane = lax.broadcasted_iota(jnp.int32, (1, HD), 1)
@@ -302,15 +302,11 @@
         place[:, pl.ds(c * HD, HD)] = jnp.where(rows == piece, 1.0, 0.0).astype(BF16)
 
     def arrange_kv(g):
-        def one(step, carry):
-            cols = pl.ds(pl.multiple_of(step * 256, 256), 256)
-            home = pl.ds(pl.multiple_of(g * span + step * 256, 256), 256)
-            whole = dot(place[...], got_kv[g, :, cols]).astype(BF16)
+        for step in range(span // 256):
+            home = pl.ds(g * span + step * 256, 256)
+            whole = dot(place[...], got_kv[g, :, pl.ds(step * 256, 256)]).astype(BF16)
             k_all[pl.ds(resident, slots), home] = whole[:slots]
             v_all[pl.ds(resident, slots), home] = whole[slots:]
-            return carry
-
-        lax.fori_loop(0, span // 256, one, 0)
 
     def first_copy(g, step):
         mate = lax.rem(p + step, plane)
@@ -361,7 +357,7 @@
                 end[h * GROUPS + m] = state[m * piece_rows : (m + 1) * piece_rows]
             return carry
 
-        lax.fori_loop(0, heads_in, one, 0, unroll=2)
+        lax.fori_loop(0, heads_in, one, 0, unroll=4)
         start_range(functools.partial(first_copy, g), 1, plane)
         in1[g * plane] = end[g * plane + p]
 
@@ -425,7 +421,7 @@
 
     def finish_group(g):
         all_third(g).wait_recv()
-        lax.fori_loop(g * heads_in, (g + 1) * heads_in, finish_resident, 0, unroll=2)
+        lax.fori_loop(g * heads_in, (g + 1) * heads_in, finish_resident, 0, unroll=4)
 
     def finish_admitted(h, carry):
         rate = rate_ref[h]
@@ -447,22 +443,20 @@
     all_kv(0).wait_recv()
     arrange_kv(0)
     ends(0)
-    start_range(kv_second, (3 * n) // 8, (5 * n) // 8)
+    start_range(kv_second, (3 * n) // 4, n)
     totals(0, rates[0])
-    start_range(kv_second, (5 * n) // 8, (13 * n) // 16)
+    start_range(q_first, 1, n // 2)
     prefixes(0, rates[0])
-    start_range(kv_second, (13 * n) // 16, n)
-    start_range(q_first, 1, n // 2)
+    start_range(q_first, n // 2, n)
 
     all_kv(1).wait_recv()
     arrange_kv(1)
     ends(1)
-    start_range(q_first, n // 2, n)
+    start_range(q_second, 1, n // 2)
     finish_group(0)
     totals(1, rates[1])
-    start_range(q_second, 1, n // 2)
+    start_range(q_second, n // 2, n)
     prefixes(1, rates[1])
-    start_range(q_second, n // 2, n)
     finish_new(0)
     finish_group(1)
     rows_in = pl.ds(0, resident)

time: 95.3 us -> 95.2 us (level)
  no operation moved by 1% of the time
where the time goes in v7:
time: 95.2 us; the launch traced here: 95.1 us
  Pallas kernels  95.1 us (100%)
    pallas_call x1, Pallas kernels, body(): pl.pallas_call(functools.partial(kernel, n, heads), out_shape=jax.ShapeDt...  92.7 us
    pallas_call x1, Pallas kernels, body(): pl.pallas_call(functools.partial(hand_over, parts), out_shape=jax.ShapeDt...  2.39 us

profile of v7, /device:TPU:1, one launch (start us, length us, event | category | flops | bytes accessed | tf_op | source)
XLA Modules:
  0.0 95.1 jit_solution(17320552838430944135)
XLA Ops:
  0.0 92.7 %shard_map.100.src = bf16[1024,1024]{1,0:T(8,128)(2,1)} custom-call(bf16[768,1024]{1,0:T(8,128)(2,1)} %q_res.1, bf16[768,1024]{1,0:T(8,128)(2,1)} %k_res.1, bf16[768,1024]{1,0:T(8,128)(2,1)} %v_res.1, bf16[256,1024]{1,0:T(8,128)(2,1)} %q_new.1, bf16[256,1024]{1,0:T(8,128)(2,1)} %k_new.1, bf16[256,1024]{1,0:T(8,128)(2,1)} %v_new.1, s32[32]{0:T(128)} %dest_ref.1, ...), custom_call_target="tpu_custom_call" | custom-call | tf_op jit(solution)/shard_map/pallas_call | solution.py:514
  92.7 2.4 %shard_map.101 = bf16[1024,1024]{1,0:T(8,128)(2,1)} custom-call(bf16[1024,1024]{1,0:T(8,128)(2,1)} %shard_map.100.src), custom_call_target="tpu_custom_call" | custom-call | tf_op jit(solution)/shard_map/pallas_call | solution.py:560

commit v8 on v7

--- a/solution.py
+++ b/solution.py
@@ -45,8 +45,8 @@
     n, plane, q_res, k_res, v_res, q_new, k_new, v_new, dest_ref, slot_ref, bound_ref, rate_ref, out,
     send_row, labels, b_row, b_col,
     q_all, k_all, v_all, kv_stack, q_stack, pay_kv, pay_q, got_kv, got_q, got_labels, place,
-    mask, alive, keep, o_local, s_local, end, in1, total, in2, before, out3, in3, done,
-    load_sem, send_sem, recv_sem, send2, recv2, out_sem,
+    mask, alive, keep, o_local, s_local, end, in1, total, in2, before, out3, in3, done, own_total, lower_sum, in4,
+    load_sem, send_sem, recv_sem, send2, recv2, out_sem, send4, recv4,
 ):
     me = lax.axis_index("seq")
     z, p = me // plane, lax.rem(me, plane)
@@ -308,6 +308,9 @@
             k_all[pl.ds(resident, slots), home] = whole[:slots]
             v_all[pl.ds(resident, slots), home] = whole[slots:]
 
+    side_z = depth // 2
+    zl = lax.rem(z, side_z)
+
     def first_copy(g, step):
         mate = lax.rem(p + step, plane)
         return pltpu.make_async_remote_copy(
@@ -328,8 +331,18 @@
         return pltpu.make_async_remote_copy(
             src_ref=total.at[g], dst_ref=in2.at[g * depth + step],
             send_sem=send2.at[g * depth + step], recv_sem=recv2.at[g * depth + step],
-            device_id={"seq": lax.rem(me + step * plane, n)}, device_id_type=MESH,
-        )
+            device_id={"seq": (z - zl + lax.rem(zl + step, side_z)) * plane + p}, device_id_type=MESH,
+        )
+
+    def lower_copy(g, u):
+        return pltpu.make_async_remote_copy(
+            src_ref=lower_sum.at[g], dst_ref=in4.at[g],
+            send_sem=send4.at[g * side_z + u], recv_sem=recv4.at[g],
+            device_id={"seq": (side_z + u) * plane + p}, device_id_type=MESH,
+        )
+
+    def lower_sender(u):
+        return side_z - 1 if 2 * u < side_z else 0
 
     def all_first(g):
         pieces = pl.ds(g * plane + 1, plane - 1)
@@ -370,21 +383,45 @@
             pass_on = decay_of(-rate_p * length) * clear(shard * length, (shard + 1) * length)
             state = pass_on * state + in1[g * plane + lax.rem(p - m + plane, plane)]
         total[g] = state.astype(BF16)
-        for step in range(1, depth):
-            @pl.when(z + step < depth)
-            def _(step=step):
-                second_copy(g, step).start()
+        own_total[g] = state
+        for step in range(1, side_z):
+            second_copy(g, step).start()
 
     def prefixes(g, rate_p):
         before[...] = jnp.zeros((piece_rows, HD), F32)
-        for step in range(1, depth):
-            @pl.when(z - step >= 0)
+        for step in range(1, side_z):
+            second_copy(g, step).wait_recv()
+        for u in sorted({lower_sender(u): u for u in range(side_z)}.values()):
+            @pl.when(z == lower_sender(u))
+            def _(u=u):
+                whole = jnp.zeros((piece_rows, HD), F32)
+                for step in range(side_z):
+                    source = lax.rem(z - step + side_z, side_z)
+                    value = own_total[g] if step == 0 else in2[g * depth + step].astype(F32)
+                    away = (plane_rows * (side_z - 1 - source)).astype(F32)
+                    factor = decay_of(-rate_p * away) * clear(
+                        (source + 1) * plane_rows, side_z * plane_rows
+                    )
+                    whole = whole + factor * value
+                lower_sum[g] = whole
+                for other in range(side_z):
+                    if lower_sender(other) == lower_sender(u):
+                        lower_copy(g, other).start()
+        for step in range(1, side_z):
+            @pl.when(zl - step >= 0)
             def _(step=step):
-                second_copy(g, step).wait_recv()
                 factor = decay_of(-rate_p * float(plane_rows * (step - 1))) * clear(
                     (z - step + 1) * plane_rows, z * plane_rows
                 )
                 before[...] = before[...] + factor * in2[g * depth + step].astype(F32)
+
+        @pl.when(z >= side_z)
+        def _():
+            lower_copy(g, 0).wait_recv()
+            away = (plane_rows * zl).astype(F32)
+            factor = decay_of(-rate_p * away) * clear(side_z * plane_rows, z * plane_rows)
+            before[...] = before[...] + factor * in4[g]
+
         earlier = before[...]
         for m in range(plane):
             factor = decay_of(-rate_p * float(length * m)) * clear(
@@ -473,10 +510,12 @@
         all_q(g).wait_send()
         all_first(g).wait_send()
         all_third(g).wait_send()
-        for step in range(1, depth):
-            @pl.when(z + step < depth)
-            def _(g=g, step=step):
-                second_copy(g, step).wait_send()
+        for step in range(1, side_z):
+            second_copy(g, step).wait_send()
+        for u in range(side_z):
+            @pl.when(z == lower_sender(u))
+            def _(g=g, u=u):
+                lower_copy(g, u).wait_send()
     store.wait()
     store_new.wait()
 
@@ -545,12 +584,17 @@
             pltpu.VMEM((GROUPS * heads, HD // GROUPS, HD), F32),
             pltpu.VMEM((GROUPS * heads, HD // GROUPS, HD), F32),
             pltpu.VMEM((length, columns), BF16),
+            pltpu.VMEM((GROUPS, HD // GROUPS, HD), F32),
+            pltpu.VMEM((GROUPS, HD // GROUPS, HD), F32),
+            pltpu.VMEM((GROUPS, HD // GROUPS, HD), F32),
             pltpu.SemaphoreType.DMA((5 + 2 * GROUPS,)),
             pltpu.SemaphoreType.DMA((4 + 3 * GROUPS,)),
             pltpu.SemaphoreType.DMA((4 + 3 * GROUPS,)),
             pltpu.SemaphoreType.DMA((GROUPS * (n // heads),)),
             pltpu.SemaphoreType.DMA((GROUPS * (n // heads),)),
             pltpu.SemaphoreType.DMA((2,)),
+            pltpu.SemaphoreType.DMA((GROUPS * (n // heads // 2),)),
+            pltpu.SemaphoreType.DMA((GROUPS,)),
         ],
         compiler_params=pltpu.CompilerParams(
             collective_id=0, has_side_effects=True, vmem_limit_bytes=60 * 1024 * 1024

time: 95.2 us -> 96.7 us (1.016)
  Pallas kernels: 95.1 us -> 96.6 us
    pallas_call x1, Pallas kernels: 92.7 us -> 94.2 us  [body(): pl.pallas_call(functools.partial(kernel, n, heads), out_shape=jax.ShapeDt...]
where the time goes in v8:
time: 96.7 us; the launch traced here: 96.6 us
  Pallas kernels  96.6 us (100%)
    pallas_call x1, Pallas kernels, body(): pl.pallas_call(functools.partial(kernel, n, heads), out_shape=jax.ShapeDt...  94.2 us
    pallas_call x1, Pallas kernels, body(): pl.pallas_call(functools.partial(hand_over, parts), out_shape=jax.ShapeDt...  2.39 us

profile of v8, /device:TPU:1, one launch (start us, length us, event | category | flops | bytes accessed | tf_op | source)
XLA Modules:
  0.0 96.6 jit_solution(952876545876730936)
XLA Ops:
  0.0 94.2 %shard_map.100.src = bf16[1024,1024]{1,0:T(8,128)(2,1)} custom-call(bf16[768,1024]{1,0:T(8,128)(2,1)} %q_res.1, bf16[768,1024]{1,0:T(8,128)(2,1)} %k_res.1, bf16[768,1024]{1,0:T(8,128)(2,1)} %v_res.1, bf16[256,1024]{1,0:T(8,128)(2,1)} %q_new.1, bf16[256,1024]{1,0:T(8,128)(2,1)} %k_new.1, bf16[256,1024]{1,0:T(8,128)(2,1)} %v_new.1, s32[32]{0:T(128)} %dest_ref.1, ...), custom_call_target="tpu_custom_call" | custom-call | tf_op jit(solution)/shard_map/pallas_call | solution.py:553
  94.2 2.4 %shard_map.101 = bf16[1024,1024]{1,0:T(8,128)(2,1)} custom-call(bf16[1024,1024]{1,0:T(8,128)(2,1)} %shard_map.100.src), custom_call_target="tpu_custom_call" | custom-call | tf_op jit(solution)/shard_map/pallas_call | solution.py:604

commit v9 on v7

--- a/solution.py
+++ b/solution.py
@@ -419,9 +419,12 @@
             finish(c, h, rate, o_local[pl.ds(c * CHUNK, CHUNK), cols])
         return carry
 
+    def finish_heads(low, high):
+        lax.fori_loop(low, high, finish_resident, 0, unroll=high - low)
+
     def finish_group(g):
         all_third(g).wait_recv()
-        lax.fori_loop(g * heads_in, (g + 1) * heads_in, finish_resident, 0, unroll=4)
+        finish_heads(g * heads_in, (g + 1) * heads_in)
 
     def finish_admitted(h, carry):
         rate = rate_ref[h]
@@ -453,9 +456,11 @@
     arrange_kv(1)
     ends(1)
     start_range(q_second, 1, n // 2)
-    finish_group(0)
+    all_third(0).wait_recv()
+    finish_heads(0, heads_in // 2)
     totals(1, rates[1])
     start_range(q_second, n // 2, n)
+    finish_heads(heads_in // 2, heads_in)
     prefixes(1, rates[1])
     finish_new(0)
     finish_group(1)

time: 95.2 us -> 95.2 us (level)
  no operation moved by 1% of the time
where the time goes in v9:
time: 95.2 us; the launch traced here: 95.1 us
  Pallas kernels  95.1 us (100%)
    pallas_call x1, Pallas kernels, body(): pl.pallas_call(functools.partial(kernel, n, heads), out_shape=jax.ShapeDt...  92.7 us
    pallas_call x1, Pallas kernels, body(): pl.pallas_call(functools.partial(hand_over, parts), out_shape=jax.ShapeDt...  2.39 us

profile of v9, /device:TPU:1, one launch (start us, length us, event | category | flops | bytes accessed | tf_op | source)
XLA Modules:
  0.0 95.1 jit_solution(14522407769721500898)
XLA Ops:
  0.0 92.7 %shard_map.100.src = bf16[1024,1024]{1,0:T(8,128)(2,1)} custom-call(bf16[768,1024]{1,0:T(8,128)(2,1)} %q_res.1, bf16[768,1024]{1,0:T(8,128)(2,1)} %k_res.1, bf16[768,1024]{1,0:T(8,128)(2,1)} %v_res.1, bf16[256,1024]{1,0:T(8,128)(2,1)} %q_new.1, bf16[256,1024]{1,0:T(8,128)(2,1)} %k_new.1, bf16[256,1024]{1,0:T(8,128)(2,1)} %v_new.1, s32[32]{0:T(128)} %dest_ref.1, ...), custom_call_target="tpu_custom_call" | custom-call | tf_op jit(solution)/shard_map/pallas_call | solution.py:519
  92.7 2.4 %shard_map.101 = bf16[1024,1024]{1,0:T(8,128)(2,1)} custom-call(bf16[1024,1024]{1,0:T(8,128)(2,1)} %shard_map.100.src), custom_call_target="tpu_custom_call" | custom-call | tf_op jit(solution)/shard_map/pallas_call | solution.py:565
